TPU v7x, 512 devices: a whole 4x4x16 slice. The times are simulated.
512 devices in a mesh: dp: 32 (over y, x, core), query: 16 (over z).
Axes of the slice: x: 4, y: 4, z: 16, core: 2. Of those that a mesh axis runs over, the one named last changes fastest.
Arguments:
- hidden_acts: bfloat16 [65536, 14336], P('dp', 'query'), may hold values from -40 to 40
- out_grads: bfloat16 [65536, 4096], P('dp', 'query'), may hold values from -40 to 40
- proj_in: bfloat16 [14336, 32], P('query')
- proj_out: bfloat16 [4096, 32], P('query')
- query_codes: float32 [1024, 1024], P('query'), may hold values from -6 to 6
Outputs:
- scores: float32 [65536, 1024], P(('dp', 'query'))
All inputs are finite; a program needn't handle non-finite values.
Results may differ from a plain program's by a relative error of at most 0.0003.
Values sent between devices are 32-bit elements; how exact they have to be, the bound alone decides.
A program may use at most 64 MiB of HBM per device.

v0:
```python
import jax
import jax.numpy as jnp
from jax import lax
from jax.sharding import PartitionSpec as P

damping = 0.1


def right_solve(factor, matrix):
    halfway = lax.linalg.triangular_solve(
        factor, matrix, left_side=False, lower=True, transpose_a=True
    )
    return lax.linalg.triangular_solve(
        factor, halfway, left_side=False, lower=True, transpose_a=False
    )


def prepare(query_block, low_in, low_out):
    code_count = query_block.shape[0]
    code_width = low_in.shape[0]
    blocks = query_block.reshape(code_count * code_width, code_width)
    right_done = right_solve(low_in, blocks).reshape(code_count, code_width, code_width)
    flipped = jnp.swapaxes(right_done, 1, 2).reshape(code_count * code_width, code_width)
    both_done = right_solve(low_out, flipped).reshape(code_count, code_width, code_width)
    return jnp.swapaxes(both_done, 1, 2).reshape(code_count, code_width * code_width)


def gram(matrix):
    return jnp.dot(
        matrix.T, matrix, precision=lax.Precision.HIGHEST, preferred_element_type=jnp.float32
    )


def outer_codes(grads_rows, acts_rows):
    code_width = acts_rows.shape[1]
    return (grads_rows[:, :, None] * acts_rows[:, None, :]).reshape(
        acts_rows.shape[0], code_width * code_width
    )


def score_against(token_codes, query_block, code_width):
    product = lax.dot_general(
        token_codes,
        query_block,
        (((1,), (1,)), ((), ())),
        precision=lax.Precision.HIGHEST,
        preferred_element_type=jnp.float32,
    )
    return product / code_width


def body(hidden_acts, out_grads, proj_in, proj_out, query_codes):
    code_width = proj_in.shape[1]
    part_acts = jnp.dot(hidden_acts, proj_in, preferred_element_type=jnp.float32)
    part_grads = jnp.dot(out_grads, proj_out, preferred_element_type=jnp.float32)
    group_count = lax.axis_size("dp")
    query_count = lax.axis_size("query")
    position = lax.axis_index("query")
    group_rows = hidden_acts.shape[0]
    own_rows = group_rows // query_count
    token_total = float(group_rows * group_count)
    acts_group, grads_group = lax.psum((part_acts, part_grads), "query")
    fisher_in, fisher_out = lax.psum((gram(acts_group), gram(grads_group)), "dp")
    acts_own = lax.dynamic_slice_in_dim(acts_group, position * own_rows, own_rows, 0)
    grads_own = lax.dynamic_slice_in_dim(grads_group, position * own_rows, own_rows, 0)
    identity = jnp.eye(code_width, dtype=jnp.float32)
    low_in = jnp.linalg.cholesky(fisher_in / token_total + damping * identity)
    low_out = jnp.linalg.cholesky(fisher_out / token_total + damping * identity)
    token_codes = outer_codes(grads_own, acts_own)
    prepared = prepare(query_codes, low_in, low_out)
    return score_against(
        token_codes, lax.all_gather(prepared, "query", axis=0, tiled=True), code_width
    )


def solution(mesh):
    return jax.shard_map(
        body,
        mesh=mesh,
        in_specs=(
            P("dp", "query"),
            P("dp", "query"),
            P("query", None),
            P("query", None),
            P("query", None),
        ),
        out_specs=P(("dp", "query"), None),
        check_vma=False,
    )
```

profile of v0, /device:TPU:4, one launch (start us, length us, event | category | flops | bytes accessed | tf_op | source)
XLA Modules:
  0.0 384.5 jit_solution(15834158124573159541)
XLA Ops:
  6.5 0.0 copy-start
  6.5 0.0 copy-start.2
  6.5 0.0 copy-start.1
  6.5 0.0 all-reduce.4.cloned.1.call-start
  6.5 4.0 %fusion.9 = f32[2048,32]{0,1:T(8,128)} fusion(bf16[2048,896]{1,0:T(8,128)(2,1)} %param.10, bf16[896,32]{0,1:T(8,128)(2,1)} %param.12), kind=kOutput, calls=%fused_computation.30 | convolution fusion | flops 117440512 | bytes 3989504 | tf_op jit(solution)/shard_map/dot_general | solution.py:54
  10.6 0.0 copy-done
  10.6 0.0 copy-done.2
  10.6 1.1 fusion.8
  11.7 0.0 all-reduce.4.cloned.1.call-update
  11.7 0.0 all-gather.2.cloned.1.call-start
  11.8 0.0 copy-done.1
  11.8 0.3 reshape.38
  12.1 141.2 %all-reduce.4.cloned.1.call-done = (f32[2048,32]{0,1:T(8,128)}, f32[2048,32]{0,1:T(8,128)}) async-done(((f32[2048,32]{0,1:T(8,128)}, f32[2048,32]{0,1:T(8,128)}), (f32[2048,32]{0,1:T(8,128)}, f32[2048,32]{0,1:T(8,128)})) %all-reduce.4.cloned.1.call-update) | async-done | bytes 524304 | tf_op jit(solution)/shard_map/psum | solution.py:62
  153.4 1.4 fusion.11
  154.7 1.4 fusion.10
  156.1 113.7 %all-reduce = (f32[32,32]{0,1:T(8,128)S(1)}, f32[32,32]{0,1:T(8,128)S(1)}) all-reduce(f32[32,32]{0,1:T(8,128)S(1)} %fusion.11, f32[32,32]{0,1:T(8,128)S(1)} %fusion.10), channel_id=1, replica_groups=mesh['dp'=32,'query'=16] {'dp'}, use_global_device_ids=true, to_apply=%region_5.7 | all-reduce | flops 2048 | bytes 16384 | tf_op jit(solution)/shard_map/psum | solution.py:63
  269.9 0.1 copy.21
  270.0 2.9 cholesky.55
  272.9 0.6 compare_reduce_fusion
  273.6 0.7 fusion.1
  274.2 2.4 custom-call.11
  276.7 0.1 copy.19
  276.8 2.9 cholesky.44
  279.7 0.6 compare_reduce_fusion.1
  280.4 0.7 fusion
  281.0 2.4 custom-call.13
  283.5 1.2 convolution_bitcast_fusion.3
  284.7 0.4 convolution_bitcast_fusion.2
  285.0 0.3 reshape.39
  285.4 1.1 copy.22
  286.5 0.5 reshape.40
  287.0 0.4 convolution_bitcast_fusion.1
  287.4 0.3 convolution_bitcast_fusion
  287.7 0.3 reshape.41
  288.1 0.3 copy.23
  288.4 0.9 copy.24
  289.3 0.0 all-gather.2.cloned.1.call-update
  289.3 0.7 constant_dynamic-slice_fusion
  290.1 0.1 broadcast_multiply_fusion
  290.1 80.0 %all-gather.2.cloned.1.call-done = f32[1024,1024]{1,0:T(8,128)} async-done(((f32[64,1024]{1,0:T(8,128)}), f32[1024,1024]{1,0:T(8,128)}) %all-gather.2.cloned.1.call-update) | async-done | bytes 4194320 | tf_op jit(solution)/shard_map/all_gather | solution.py:72
  370.2 7.5 %convolution_multiply_fusion = f32[128,1024]{1,0:T(8,128)} fusion(f32[128,1024]{0,1:T(8,128)S(1)} %bitcast.60, f32[1024,1024]{1,0:T(8,128)} %all-gather.2.cloned.1.call-done), kind=kOutput, calls=%fused_computation.4 | convolution fusion | flops 1610743808 | bytes 5242880 | tf_op jit(solution)/shard_map/dot_general | solution.py:42
  (5 shorter events, 0.1 us)
Async XLA Ops:
  6.5 4.1 %copy-start = (bf16[2048,256]{1,0:T(8,128)(2,1)S(1)}, bf16[2048,256]{1,0:T(8,128)(2,1)}, u32[]{:S(2)}) copy-start(bf16[2048,256]{1,0:T(8,128)(2,1)} %param.11) | copy-start | bytes 3145732
  6.5 4.1 %copy-start.2 = (bf16[256,32]{0,1:T(8,128)(2,1)S(1)}, bf16[256,32]{0,1:T(8,128)(2,1)}, u32[]{:S(2)}) copy-start(bf16[256,32]{0,1:T(8,128)(2,1)} %param.13) | copy-start | bytes 49156
  6.5 5.2 %copy-start.1 = (f32[64,1024]{1,0:T(8,128)S(1)}, f32[64,1024]{1,0:T(8,128)}, u32[]{:S(2)}) copy-start(f32[64,1024]{1,0:T(8,128)} %param.14) | copy-start | bytes 786436
  6.5 146.8 %all-reduce.4.cloned.1.call-start = ((), (), s32[]{:S(2)}) async-start(), calls=%async_computation.1 | async-start | bytes 1048576 | tf_op jit(solution)/shard_map/psum | solution.py:62
  11.7 358.4 %all-gather.2.cloned.1.call-start = ((), (), s32[]{:S(2)}) async-start(), calls=%async_computation | async-start | bytes 4456448 | tf_op jit(solution)/shard_map/all_gather | solution.py:72
Sparse Core Ops, SparseCore 0:
  11.8 141.4 all-reduce.3
  289.4 80.6 all-gather.1
where the time goes:
time: 385 us; the launch traced here: 384 us
  waiting for transfers between devices  221 us (57%)
  blocking collectives  114 us (30%)
  matrix products  17.7 us (5%)
  other arithmetic  13.5 us (4%)
  between operations  13.5 us (4%)
  local copies, waits for them, and re-layouts  4.7 us (1%)
    psum x1, waiting for transfers between devices, body(): acts_group, grads_group = lax.psum((part_acts, part_grads), 'query')  141 us
    psum x1, blocking collectives, body(): lax.psum((gram(acts_group), gram(grads_group)), 'dp')  114 us
    all_gather x1, waiting for transfers between devices, body(): lax.all_gather(prepared, 'query', axis=0, tiled=True)  80 us
  transfers between devices with their start and end apart: 2, of which 2 were waited for; matrix products, arithmetic and copies ran while one was open for 0% of the time, Pallas kernels for 0%

commit v1 on v0

v1 whole, which is shorter than its diff:
```python
import jax
import jax.numpy as jnp
from jax import lax
from jax.experimental import pallas as pl
from jax.experimental.pallas import tpu as pltpu
from jax.sharding import PartitionSpec as P

damping = 0.1
MESH = pl.DeviceIdType.MESH
HIGHEST = lax.Precision.HIGHEST
f32 = jnp.float32
bf16 = jnp.bfloat16


def dot_nt(a, b, precision=None):
    return lax.dot_general(
        a, b, (((1,), (1,)), ((), ())), precision=precision, preferred_element_type=f32
    )


def dot_nn(a, b, precision=None):
    return lax.dot_general(
        a, b, (((1,), (0,)), ((), ())), precision=precision, preferred_element_type=f32
    )


def dot_tn(a, b, precision=None):
    return lax.dot_general(
        a, b, (((0,), (0,)), ((), ())), precision=precision, preferred_element_type=f32
    )


def iota(shape, axis):
    return lax.broadcasted_iota(jnp.int32, shape, axis)


def tile_lanes(x, start):
    lane = iota(x.shape, 1)
    kept = jnp.where((lane >= start) & (lane < start + 32), x, 0.0)
    twice = kept + pltpu.roll(kept, 32, 1)
    return twice + pltpu.roll(twice, 64, 1)


def pack(square):
    lane = iota((8, 128), 1) // 32
    tile = square[0:8]
    for k in range(1, 4):
        tile = jnp.where(lane == k, square[8 * k : 8 * k + 8], tile)
    return tile


def unpack(tile):
    rows = [tile] + [pltpu.roll(tile, 128 - 32 * k, 1) for k in range(1, 4)]
    return jnp.concatenate(rows, axis=0)


def inverse(matrix):
    lane = iota((32, 128), 1)
    row_id = iota((32, 128), 0)
    for k in range(32):
        pivot = 1.0 / matrix[k : k + 1, k : k + 1]
        row = jnp.where(lane[0:1] == k, 1.0, matrix[k : k + 1, :]) * pivot
        column = jnp.where(row_id == k, -1.0, matrix[:, k : k + 1])
        base = jnp.where((lane == k) | (row_id == k), 0.0, matrix)
        matrix = base - column * row
    return matrix


def kernel(
    tokens, hid, grd, wi, wo, codes, out,
    hbuf, gbuf, wip, wop, part, from_left, from_right, eighth, second, third,
    fsend, fpair, ftile, fz, zsum, fp, minv, mpair, q, qhi, qlo, expand, chi, clo,
    load_sem, qload_sem, rs_send, rs_recv, f_send, f_recv,
    qz_send, qz_recv, qp_send, qp_recv, qc_send, qc_recv,
):
    dp = lax.axis_index("dp")
    z = lax.axis_index("query")
    core = lax.rem(dp, 2)
    sibling = dp + 1 - 2 * core

    def at_z(offset):
        return lax.rem(z + offset + 16, 16)

    def chip(i):
        return lax.rem(dp + 2 * i, 32)

    def remote(src, dst, ss, rs, device):
        return pltpu.make_async_remote_copy(
            src_ref=src, dst_ref=dst, send_sem=ss, recv_sem=rs,
            device_id=device, device_id_type=MESH,
        )

    loads = []
    for g in range(4):
        rows = pl.ds(512 * g, 512)
        loads.append((
            pltpu.make_async_copy(hid.at[rows, :], hbuf.at[rows, :], load_sem.at[g, 0]),
            pltpu.make_async_copy(grd.at[rows, :], gbuf.at[rows, :], load_sem.at[g, 1]),
        ))
        loads[-1][0].start()
        loads[-1][1].start()

    def q_rows(which):
        return pl.ds(pl.multiple_of((which // 4) * 8, 8), 8)

    def q_lanes(which):
        return pl.ds(pl.multiple_of(lax.rem(which, 4) * 256, 256), 256)

    own_q = pltpu.make_async_copy(
        codes.at[q_rows(dp), q_lanes(dp)], q.at[z, q_rows(dp), q_lanes(dp)], qload_sem
    )
    own_q.start()

    barrier = pltpu.get_barrier_semaphore()

    def hello_z(i, carry):
        pl.semaphore_signal(barrier, inc=1, device_id=(dp, at_z(i)), device_id_type=MESH)
        return carry

    def hello_chip(i, carry):
        pl.semaphore_signal(barrier, inc=1, device_id=(chip(i), z), device_id_type=MESH)
        return carry

    lax.fori_loop(1, 16, hello_z, 0)
    lax.fori_loop(1, 16, hello_chip, 0)
    pl.semaphore_signal(barrier, inc=1, device_id=(sibling, z), device_id_type=MESH)

    wip[...] = jnp.zeros_like(wip)
    wop[...] = jnp.zeros_like(wop)
    wip[0, 0:32, :] = wi[...]
    wip[1, 64:96, :] = wi[...]
    wop[0, 32:64, :] = wo[...]
    wop[1, 96:128, :] = wo[...]
    for g in range(4):
        loads[g][0].wait()
        loads[g][1].wait()
        total = None
        for half in range(2):
            starts = [512 * g + 128 * j + 64 * half for j in range(4)]
            h = jnp.concatenate([hbuf[s : s + 64, :] for s in starts], axis=0)
            o = jnp.concatenate([gbuf[s : s + 64, :] for s in starts], axis=0)
            term = dot_nt(h, wip[half]) + dot_nt(o, wop[half])
            total = term if total is None else total + term
        part[4 * g : 4 * g + 4] = total.reshape(4, 64, 128)

    expand[...] = jnp.where(
        iota((128, 1024), 1) // 32 == iota((128, 1024), 0), 1.0, 0.0
    ).astype(bf16)

    own_q.wait()
    pl.semaphore_wait(barrier, 31)

    stage1 = []
    for m in (2, -2, 1, -1, 0):
        i = m + 2
        right = remote(part.at[at_z(3 * m + 1)], from_left.at[i],
                       rs_send.at[i], rs_recv.at[i], (dp, at_z(1)))
        left = remote(part.at[at_z(3 * m - 1)], from_right.at[i],
                      rs_send.at[5 + i], rs_recv.at[5 + i], (dp, at_z(-1)))
        right.start()
        left.start()
        stage1 += [right, left]
        if abs(m) == 2:
            s = 0 if m == 2 else 1
            far = remote(part.at[at_z(8), pl.ds(32 * s, 32), :], eighth.at[s],
                         rs_send.at[10 + s], rs_recv.at[10 + s],
                         (dp, at_z(2 if m == 2 else -2)))
            far.start()
            stage1.append(far)
    hub2r, hub2l, far_up, hub_2r, hub_2l, far_down, hub1r, hub1l, hub_1r, hub_1l, hub0r, hub0l = stage1

    def send_qz(i, carry):
        remote(q.at[z, q_rows(dp), q_lanes(dp)], q.at[z, q_rows(dp), q_lanes(dp)],
               qz_send.at[i], qz_recv.at[i], (dp, at_z(i))).start()
        return carry

    lax.fori_loop(1, 16, send_qz, 0)

    hub2r.wait_recv()
    hub2l.wait_recv()
    far_up.wait_recv()
    part[at_z(6)] = part[at_z(6)] + from_left[4] + from_right[4]
    part[at_z(6), 0:32, :] = part[at_z(6), 0:32, :] + eighth[0]
    up2 = remote(part.at[at_z(6)], second.at[0], rs_send.at[12], rs_recv.at[12], (dp, at_z(3)))
    up2.start()
    hub_2r.wait_recv()
    hub_2l.wait_recv()
    far_down.wait_recv()
    part[at_z(-6)] = part[at_z(-6)] + from_left[0] + from_right[0]
    part[at_z(-6), 32:64, :] = part[at_z(-6), 32:64, :] + eighth[1]
    down2 = remote(part.at[at_z(-6)], second.at[1], rs_send.at[13], rs_recv.at[13], (dp, at_z(-3)))
    down2.start()

    hub1r.wait_recv()
    hub1l.wait_recv()
    hub_1r.wait_recv()
    hub_1l.wait_recv()
    up = part[at_z(3)] + from_left[3] + from_right[3]
    down = part[at_z(-3)] + from_left[1] + from_right[1]
    hub0r.wait_recv()
    hub0l.wait_recv()
    mine = part[z] + from_left[2] + from_right[2]

    up2.wait_recv()
    part[at_z(3)] = up + second[0]
    up3 = remote(part.at[at_z(3)], third.at[0], rs_send.at[14], rs_recv.at[14], (dp, at_z(3)))
    up3.start()
    down2.wait_recv()
    part[at_z(-3)] = down + second[1]
    down3 = remote(part.at[at_z(-3)], third.at[1], rs_send.at[15], rs_recv.at[15], (dp, at_z(-3)))
    down3.start()

    def wait_qz(i, carry):
        remote(q.at[z, q_rows(dp), q_lanes(dp)], q.at[at_z(-i), q_rows(dp), q_lanes(dp)],
               qz_send.at[i], qz_recv.at[i], (dp, at_z(i))).wait()
        return carry

    lax.fori_loop(1, 16, wait_qz, 0)

    def q_block(which):
        return q.at[:, q_rows(which), q_lanes(which)]

    def send_qp(i, carry):
        remote(q_block(dp), q_block(dp), qp_send.at[i], qp_recv.at[i], (chip(i), z)).start()
        return carry

    lax.fori_loop(1, 16, send_qp, 0)

    up3.wait_recv()
    down3.wait_recv()
    x = mine + third[0] + third[1]

    acts4 = jnp.concatenate([tile_lanes(x, 0), tile_lanes(x, 64)], axis=0)
    grads4 = jnp.concatenate([tile_lanes(x, 32), tile_lanes(x, 96)], axis=0)
    fin = pack(dot_tn(acts4, acts4, HIGHEST)[0:32])
    fout = pack(dot_tn(grads4, grads4, HIGHEST)[0:32])
    first_core = core == 0
    fsend[...] = jnp.where(first_core, fout, fin)
    pair = remote(fsend, fpair, f_send.at[0], f_recv.at[0], (sibling, z))
    pair.start()
    keep = jnp.where(first_core, fin, fout)
    pair.wait_recv()
    ftile[...] = keep + fpair[...]

    def send_fz(i, carry):
        j = lax.rem(i + 7, 15) + 1
        remote(ftile, fz.at[j], f_send.at[j], f_recv.at[j], (dp, at_z(j))).start()
        return carry

    lax.fori_loop(0, 15, send_fz, 0)

    def wait_fz(i, total):
        remote(ftile, fz.at[i], f_send.at[i], f_recv.at[i], (dp, at_z(i))).wait_recv()
        return total + fz[i]

    zsum[...] = lax.fori_loop(1, 16, wait_fz, ftile[...])

    def send_fp(i, carry):
        remote(zsum, fp.at[i], f_send.at[15 + i], f_recv.at[15 + i], (chip(i), z)).start()
        return carry

    lax.fori_loop(1, 16, send_fp, 0)

    def wait_fp(i, total):
        remote(zsum, fp.at[i], f_send.at[15 + i], f_recv.at[15 + i], (chip(i), z)).wait_recv()
        return total + fp[i]

    fisher = unpack(lax.fori_loop(1, 16, wait_fp, zsum[...]))
    eye = iota((32, 128), 0) == iota((32, 128), 1)
    fisher = fisher / tokens + jnp.where(eye, damping, 0.0)
    minv[...] = inverse(jnp.where(iota((32, 128), 1) < 32, fisher, 0.0))
    swap = remote(minv, mpair, f_send.at[31], f_recv.at[31], (sibling, z))
    swap.start()

    def q_to_core(i, carry):
        which = chip(-i + 16)
        @pl.when(i > 0)
        def _():
            remote(q_block(dp), q_block(which), qp_send.at[i], qp_recv.at[i], (chip(i), z)).wait()
        remote(q_block(which), q_block(which), qc_send.at[i], qc_recv.at[i], (sibling, z)).start()
        return carry

    lax.fori_loop(0, 16, q_to_core, 0)

    def q_from_core(i, carry):
        mate = lax.rem(sibling + 32 - 2 * i, 32)
        remote(q_block(chip(-i + 16)), q_block(mate), qc_send.at[i], qc_recv.at[i], (sibling, z)).wait()
        return carry

    lax.fori_loop(0, 16, q_from_core, 0)

    def split_q(i, carry):
        rows = pl.ds(pl.multiple_of(i * 64, 64), 64)
        block = q[i]
        high = block.astype(bf16)
        qhi[rows, :] = high
        qlo[rows, :] = (block - high.astype(f32)).astype(bf16)
        return carry

    lax.fori_loop(0, 16, split_q, 0)

    swap.wait_recv()
    mine_inv, other_inv = minv[...], mpair[...]
    inv_in = tile_lanes(jnp.where(first_core, mine_inv, other_inv), 0)
    inv_out = jnp.where(first_core, other_inv, mine_inv)
    zero = jnp.zeros((32, 128), f32)
    weights = jnp.concatenate([
        jnp.concatenate([inv_in, zero, zero, zero], axis=0),
        jnp.concatenate([zero, zero, inv_in, zero], axis=0),
        jnp.concatenate([zero, inv_out, zero, zero], axis=0),
        jnp.concatenate([zero, zero, zero, inv_out], axis=0),
    ], axis=1)
    ready = dot_nn(x, weights, HIGHEST)
    acts_ready = jnp.concatenate([ready[:, 0:128], ready[:, 128:256]], axis=0)
    grads_ready = jnp.concatenate([ready[:, 256:384], ready[:, 384:512]], axis=0) * (1.0 / 32.0)
    grads_high = grads_ready.astype(bf16)
    grads_low = (grads_ready - grads_high.astype(f32)).astype(bf16)
    for k in range(8):
        lanes = slice(128 * k, 128 * k + 128)
        wide = dot_nn(grads_high, expand[:, lanes]) + dot_nn(grads_low, expand[:, lanes])
        code = wide * acts_ready
        high = code.astype(bf16)
        chi[:, lanes] = high
        clo[:, lanes] = (code - high.astype(f32)).astype(bf16)

    def score(i, carry):
        rows = pl.ds(pl.multiple_of(i * 256, 256), 256)
        high = qhi[rows, :]
        out[:, rows] = (
            dot_nt(chi[...], high) + dot_nt(clo[...], high) + dot_nt(chi[...], qlo[rows, :])
        )
        return carry

    lax.fori_loop(0, 4, score, 0)

    for copy in stage1 + [up2, down2, up3, down3, pair, swap]:
        copy.wait_send()

    def sent(i, carry):
        remote(ftile, fz.at[i], f_send.at[i], f_recv.at[i], (dp, at_z(i))).wait_send()
        remote(zsum, fp.at[i], f_send.at[15 + i], f_recv.at[15 + i], (chip(i), z)).wait_send()
        return carry

    lax.fori_loop(1, 16, sent, 0)


def body(hidden_acts, out_grads, proj_in, proj_out, query_codes):
    tokens = float(hidden_acts.shape[0] * lax.axis_size("dp"))
    vmem = pl.BlockSpec(memory_space=pltpu.VMEM)
    any_space = pl.BlockSpec(memory_space=pl.ANY)
    dma = pltpu.SemaphoreType.DMA

    def call(*refs):
        kernel(tokens, *refs)

    return pl.pallas_call(
        call,
        out_shape=jax.ShapeDtypeStruct((128, 1024), f32),
        in_specs=[any_space, any_space, vmem, vmem, any_space],
        out_specs=vmem,
        scratch_shapes=[
            pltpu.VMEM((2048, 896), bf16),
            pltpu.VMEM((2048, 256), bf16),
            pltpu.VMEM((2, 128, 896), bf16),
            pltpu.VMEM((2, 128, 256), bf16),
            pltpu.VMEM((16, 64, 128), f32),
            pltpu.VMEM((5, 64, 128), f32),
            pltpu.VMEM((5, 64, 128), f32),
            pltpu.VMEM((2, 32, 128), f32),
            pltpu.VMEM((2, 64, 128), f32),
            pltpu.VMEM((2, 64, 128), f32),
            pltpu.VMEM((8, 128), f32),
            pltpu.VMEM((8, 128), f32),
            pltpu.VMEM((8, 128), f32),
            pltpu.VMEM((16, 8, 128), f32),
            pltpu.VMEM((8, 128), f32),
            pltpu.VMEM((16, 8, 128), f32),
            pltpu.VMEM((32, 128), f32),
            pltpu.VMEM((32, 128), f32),
            pltpu.VMEM((16, 64, 1024), f32),
            pltpu.VMEM((1024, 1024), bf16),
            pltpu.VMEM((1024, 1024), bf16),
            pltpu.VMEM((128, 1024), bf16),
            pltpu.VMEM((128, 1024), bf16),
            pltpu.VMEM((128, 1024), bf16),
            dma((4, 2)),
            dma,
            dma((16,)), dma((16,)),
            dma((32,)), dma((32,)),
            dma((16,)), dma((16,)),
            dma((16,)), dma((16,)),
            dma((16,)), dma((16,)),
        ],
        name="influence",
        compiler_params=pltpu.CompilerParams(
            collective_id=0, has_side_effects=True, vmem_limit_bytes=56 << 20
        ),
    )(hidden_acts, out_grads, proj_in.T, proj_out.T, query_codes)


def solution(mesh):
    return jax.shard_map(
        body,
        mesh=mesh,
        in_specs=(
            P("dp", "query"),
            P("dp", "query"),
            P("query", None),
            P("query", None),
            P("query", None),
        ),
        out_specs=P(("dp", "query"), None),
        check_vma=False,
    )
```

time: 385 us -> 74.7 us (0.19)
  the two profiles are of different devices: /device:TPU:4 before, /device:TPU:1 now
where the time goes in v1:
time: 74.7 us; the launch traced here: 74.5 us
  Pallas kernels  72.6 us (97%)
  local copies, waits for them, and re-layouts  1.89 us (3%)
    pallas_call x1, Pallas kernels, body(): pl.pallas_call(call, out_shape=jax.ShapeDtypeStruct((128, 1024), f32), in...  72.6 us
    unnamed x1, local copies, waits for them, and re-layouts  1.89 us

profile of v1, /device:TPU:1, one launch (start us, length us, event | category | flops | bytes accessed | tf_op | source)
XLA Modules:
  0.0 74.5 jit_solution(10327446798369540203)
XLA Ops:
  0.0 72.6 %influence.1 = f32[128,1024]{1,0:T(8,128)} custom-call(bf16[2048,896]{1,0:T(8,128)(2,1)} %refs_0_.1, bf16[2048,256]{1,0:T(8,128)(2,1)} %refs_1_.1, bf16[32,896]{1,0:T(8,128)(2,1)} %bitcast.2, bf16[32,256]{1,0:T(8,128)(2,1)} %bitcast.3, f32[64,1024]{1,0:T(8,128)} %refs_4_.1), custom_call_target="tpu_custom_call" | custom-call | tf_op jit(solution)/shard_map/influence/pallas_call | solution.py:356
  72.6 1.9 %copy.7 = f32[128,1024]{1,0:T(8,128)} copy(f32[128,1024]{1,0:T(8,128)} %influence.1) | data formatting | bytes 1048576

commit v2 on v1

--- a/solution.py
+++ b/solution.py
@@ -70,7 +70,7 @@
     tokens, hid, grd, wi, wo, codes, out,
     hbuf, gbuf, wip, wop, part, from_left, from_right, eighth, second, third,
     fsend, fpair, ftile, fz, zsum, fp, minv, mpair, q, qhi, qlo, expand, chi, clo,
-    load_sem, qload_sem, rs_send, rs_recv, f_send, f_recv,
+    weight_sem, load_sem, qload_sem, rs_send, rs_recv, f_send, f_recv,
     qz_send, qz_recv, qp_send, qp_recv, qc_send, qc_recv,
 ):
     dp = lax.axis_index("dp")
@@ -90,6 +90,17 @@
             device_id=device, device_id_type=MESH,
         )
 
+    weights_in = []
+    for half in range(2):
+        for src, dst, at in ((wi, wip, 0), (wo, wop, 32)):
+            rows = pl.ds(64 * half + at, 32)
+            weights_in.append(pltpu.make_async_copy(
+                src, dst.at[half, rows, :], weight_sem.at[len(weights_in)]
+            ))
+    wip[...] = jnp.zeros_like(wip)
+    wop[...] = jnp.zeros_like(wop)
+    for copy in weights_in:
+        copy.start()
     loads = []
     for g in range(4):
         rows = pl.ds(512 * g, 512)
@@ -101,14 +112,18 @@
         loads[-1][1].start()
 
     def q_rows(which):
-        return pl.ds(pl.multiple_of((which // 4) * 8, 8), 8)
+        return pl.ds(pl.multiple_of((which // 8) * 16, 16), 16)
 
     def q_lanes(which):
-        return pl.ds(pl.multiple_of(lax.rem(which, 4) * 256, 256), 256)
-
-    own_q = pltpu.make_async_copy(
-        codes.at[q_rows(dp), q_lanes(dp)], q.at[z, q_rows(dp), q_lanes(dp)], qload_sem
-    )
+        return pl.ds(pl.multiple_of(lax.rem(which, 8) * 128, 128), 128)
+
+    def q_piece(from_z):
+        return q.at[from_z, q_rows(dp), q_lanes(dp)]
+
+    def q_block(which):
+        return q.at[:, q_rows(which), q_lanes(which)]
+
+    own_q = pltpu.make_async_copy(codes.at[q_rows(dp), q_lanes(dp)], q_piece(z), qload_sem)
     own_q.start()
 
     barrier = pltpu.get_barrier_semaphore()
@@ -125,12 +140,8 @@
     lax.fori_loop(1, 16, hello_chip, 0)
     pl.semaphore_signal(barrier, inc=1, device_id=(sibling, z), device_id_type=MESH)
 
-    wip[...] = jnp.zeros_like(wip)
-    wop[...] = jnp.zeros_like(wop)
-    wip[0, 0:32, :] = wi[...]
-    wip[1, 64:96, :] = wi[...]
-    wop[0, 32:64, :] = wo[...]
-    wop[1, 96:128, :] = wo[...]
+    for copy in weights_in:
+        copy.wait()
     for g in range(4):
         loads[g][0].wait()
         loads[g][1].wait()
@@ -169,12 +180,11 @@
             stage1.append(far)
     hub2r, hub2l, far_up, hub_2r, hub_2l, far_down, hub1r, hub1l, hub_1r, hub_1l, hub0r, hub0l = stage1
 
-    def send_qz(i, carry):
-        remote(q.at[z, q_rows(dp), q_lanes(dp)], q.at[z, q_rows(dp), q_lanes(dp)],
-               qz_send.at[i], qz_recv.at[i], (dp, at_z(i))).start()
-        return carry
-
-    lax.fori_loop(1, 16, send_qz, 0)
+    spread = []
+    for i, offset in enumerate((3, -3, 6, -6, 8)):
+        spread.append((remote(q_piece(z), q_piece(z), qz_send.at[i], qz_recv.at[i], (dp, at_z(offset))),
+                       remote(q_piece(z), q_piece(at_z(-offset)), qz_send.at[i], qz_recv.at[i], (dp, at_z(offset)))))
+        spread[-1][0].start()
 
     hub2r.wait_recv()
     hub2l.wait_recv()
@@ -201,6 +211,16 @@
     hub0l.wait_recv()
     mine = part[z] + from_left[2] + from_right[2]
 
+    for pair in spread:
+        pair[1].wait()
+    near = []
+    for i, offset in enumerate((0, 3, -3, 6, -6)):
+        for side, base in ((1, 5), (-1, 10)):
+            held, coming = q_piece(at_z(offset)), q_piece(at_z(offset - side))
+            sems = (qz_send.at[base + i], qz_recv.at[base + i], (dp, at_z(side)))
+            near.append((remote(held, held, *sems), remote(held, coming, *sems)))
+            near[-1][0].start()
+
     up2.wait_recv()
     part[at_z(3)] = up + second[0]
     up3 = remote(part.at[at_z(3)], third.at[0], rs_send.at[14], rs_recv.at[14], (dp, at_z(3)))
@@ -210,21 +230,56 @@
     down3 = remote(part.at[at_z(-3)], third.at[1], rs_send.at[15], rs_recv.at[15], (dp, at_z(-3)))
     down3.start()
 
-    def wait_qz(i, carry):
-        remote(q.at[z, q_rows(dp), q_lanes(dp)], q.at[at_z(-i), q_rows(dp), q_lanes(dp)],
-               qz_send.at[i], qz_recv.at[i], (dp, at_z(i))).wait()
-        return carry
-
-    lax.fori_loop(1, 16, wait_qz, 0)
-
-    def q_block(which):
-        return q.at[:, q_rows(which), q_lanes(which)]
-
-    def send_qp(i, carry):
-        remote(q_block(dp), q_block(dp), qp_send.at[i], qp_recv.at[i], (chip(i), z)).start()
-        return carry
-
-    lax.fori_loop(1, 16, send_qp, 0)
+    def plane(of_core, a, b):
+        x, y = lax.rem(dp // 2, 4), dp // 8
+        dx = a * (1 - of_core) + b * of_core
+        dy = b * (1 - of_core) + a * of_core
+        return (lax.rem(y + dy + 4, 4) * 4 + lax.rem(x + dx + 4, 4)) * 2 + of_core
+
+    def index(a, b):
+        return 4 * (a % 4) + b % 4
+
+    q_sent = []
+
+    def q_pass(a, b, da, db):
+        i = index(a - da, b - db)
+        block = q_block(plane(core, a, b))
+        copy = remote(block, block, qp_send.at[i], qp_recv.at[i], (plane(core, da, db), z))
+        copy.start()
+        q_sent.append(copy)
+
+    def q_split(which):
+        for from_z in range(16):
+            block = q[from_z, q_rows(which), q_lanes(which)]
+            high = block.astype(bf16)
+            qhi[from_z, q_rows(which), q_lanes(which)] = high
+            qlo[from_z, q_rows(which), q_lanes(which)] = (block - high.astype(f32)).astype(bf16)
+
+    def q_mate(a, b):
+        block = q_block(plane(core, a, b))
+        i = index(a, b)
+        copy = remote(block, block, qc_send.at[i], qc_recv.at[i], (sibling, z))
+        copy.start()
+        q_sent.append(copy)
+
+    def q_take(a, b):
+        i = index(a, b)
+        block = q_block(plane(core, a, b))
+        remote(block, block, qp_send.at[i], qp_recv.at[i], (sibling, z)).wait_recv()
+        q_mate(a, b)
+
+    def q_take_mate(a, b):
+        i = index(a, b)
+        which = plane(1 - core, a, b)
+        remote(q_block(which), q_block(which), qc_send.at[i], qc_recv.at[i], (sibling, z)).wait_recv()
+        q_split(which)
+
+    for pair in near:
+        pair[1].wait()
+    for da, db in ((1, 0), (-1, 0), (0, 1), (0, -1), (2, 0)):
+        q_pass(0, 0, da, db)
+    q_mate(0, 0)
+    q_split(dp)
 
     up3.wait_recv()
     down3.wait_recv()
@@ -236,10 +291,10 @@
     fout = pack(dot_tn(grads4, grads4, HIGHEST)[0:32])
     first_core = core == 0
     fsend[...] = jnp.where(first_core, fout, fin)
-    pair = remote(fsend, fpair, f_send.at[0], f_recv.at[0], (sibling, z))
-    pair.start()
+    fisher_pair = remote(fsend, fpair, f_send.at[0], f_recv.at[0], (sibling, z))
+    fisher_pair.start()
     keep = jnp.where(first_core, fin, fout)
-    pair.wait_recv()
+    fisher_pair.wait_recv()
     ftile[...] = keep + fpair[...]
 
     def send_fz(i, carry):
@@ -249,6 +304,20 @@
 
     lax.fori_loop(0, 15, send_fz, 0)
 
+    for a in (1, -1):
+        q_take(a, 0)
+        q_pass(a, 0, 0, 1)
+        q_pass(a, 0, 0, -1)
+    q_take(0, -1)
+    q_pass(0, -1, 0, 1)
+    q_take(0, 1)
+    q_take(2, 0)
+    q_pass(2, 0, 0, 1)
+    q_pass(2, 0, 0, -1)
+    for a, b in ((1, 0), (-1, 0), (0, 1), (0, -1), (2, 0)):
+        q_split(plane(core, a, b))
+    q_take_mate(0, 0)
+
     def wait_fz(i, total):
         remote(ftile, fz.at[i], f_send.at[i], f_recv.at[i], (dp, at_z(i))).wait_recv()
         return total + fz[i]
@@ -260,6 +329,17 @@
         return carry
 
     lax.fori_loop(1, 16, send_fp, 0)
+
+    q_take(1, -1)
+    q_pass(1, -1, 0, 1)
+    q_take(-1, 1)
+    q_pass(-1, 1, 0, -1)
+    q_take(1, 1)
+    q_take(-1, -1)
+    for a, b in ((1, -1), (-1, 1), (1, 1), (-1, -1)):
+        q_split(plane(core, a, b))
+    for a, b in ((1, 0), (-1, 0), (0, 1), (0, -1), (2, 0)):
+        q_take_mate(a, b)
 
     def wait_fp(i, total):
         remote(zsum, fp.at[i], f_send.at[15 + i], f_recv.at[15 + i], (chip(i), z)).wait_recv()
@@ -272,32 +352,19 @@
     swap = remote(minv, mpair, f_send.at[31], f_recv.at[31], (sibling, z))
     swap.start()
 
-    def q_to_core(i, carry):
-        which = chip(-i + 16)
-        @pl.when(i > 0)
-        def _():
-            remote(q_block(dp), q_block(which), qp_send.at[i], qp_recv.at[i], (chip(i), z)).wait()
-        remote(q_block(which), q_block(which), qc_send.at[i], qc_recv.at[i], (sibling, z)).start()
-        return carry
-
-    lax.fori_loop(0, 16, q_to_core, 0)
-
-    def q_from_core(i, carry):
-        mate = lax.rem(sibling + 32 - 2 * i, 32)
-        remote(q_block(chip(-i + 16)), q_block(mate), qc_send.at[i], qc_recv.at[i], (sibling, z)).wait()
-        return carry
-
-    lax.fori_loop(0, 16, q_from_core, 0)
-
-    def split_q(i, carry):
-        rows = pl.ds(pl.multiple_of(i * 64, 64), 64)
-        block = q[i]
-        high = block.astype(bf16)
-        qhi[rows, :] = high
-        qlo[rows, :] = (block - high.astype(f32)).astype(bf16)
-        return carry
-
-    lax.fori_loop(0, 16, split_q, 0)
+    q_take(2, 1)
+    q_pass(2, 1, 0, -1)
+    q_take(2, -1)
+    q_take(0, 2)
+    q_take(1, 2)
+    q_take(-1, 2)
+    for a, b in ((2, 1), (2, -1), (0, 2), (1, 2), (-1, 2)):
+        q_split(plane(core, a, b))
+    for a, b in ((1, -1), (-1, 1), (1, 1), (-1, -1), (2, 1), (2, -1), (0, 2), (1, 2), (-1, 2)):
+        q_take_mate(a, b)
+    q_take(2, 2)
+    q_split(plane(core, 2, 2))
+    q_take_mate(2, 2)
 
     swap.wait_recv()
     mine_inv, other_inv = minv[...], mpair[...]
@@ -325,15 +392,15 @@
 
     def score(i, carry):
         rows = pl.ds(pl.multiple_of(i * 256, 256), 256)
-        high = qhi[rows, :]
-        out[:, rows] = (
-            dot_nt(chi[...], high) + dot_nt(clo[...], high) + dot_nt(chi[...], qlo[rows, :])
-        )
+        four = pl.ds(4 * i, 4)
+        high = qhi[four].reshape(256, 1024)
+        low = qlo[four].reshape(256, 1024)
+        out[:, rows] = dot_nt(chi[...], high) + dot_nt(clo[...], high) + dot_nt(chi[...], low)
         return carry
 
     lax.fori_loop(0, 4, score, 0)
 
-    for copy in stage1 + [up2, down2, up3, down3, pair, swap]:
+    for copy in stage1 + [up2, down2, up3, down3, fisher_pair, swap] + q_sent:
         copy.wait_send()
 
     def sent(i, carry):
@@ -347,7 +414,7 @@
 def body(hidden_acts, out_grads, proj_in, proj_out, query_codes):
     tokens = float(hidden_acts.shape[0] * lax.axis_size("dp"))
     vmem = pl.BlockSpec(memory_space=pltpu.VMEM)
-    any_space = pl.BlockSpec(memory_space=pl.ANY)
+    hbm = pl.BlockSpec(memory_space=pltpu.HBM)
     dma = pltpu.SemaphoreType.DMA
 
     def call(*refs):
@@ -356,7 +423,7 @@
     return pl.pallas_call(
         call,
         out_shape=jax.ShapeDtypeStruct((128, 1024), f32),
-        in_specs=[any_space, any_space, vmem, vmem, any_space],
+        in_specs=[hbm] * 5,
         out_specs=vmem,
         scratch_shapes=[
             pltpu.VMEM((2048, 896), bf16),
@@ -378,11 +445,12 @@
             pltpu.VMEM((32, 128), f32),
             pltpu.VMEM((32, 128), f32),
             pltpu.VMEM((16, 64, 1024), f32),
-            pltpu.VMEM((1024, 1024), bf16),
-            pltpu.VMEM((1024, 1024), bf16),
+            pltpu.VMEM((16, 64, 1024), bf16),
+            pltpu.VMEM((16, 64, 1024), bf16),
             pltpu.VMEM((128, 1024), bf16),
             pltpu.VMEM((128, 1024), bf16),
             pltpu.VMEM((128, 1024), bf16),
+            dma((4,)),
             dma((4, 2)),
             dma,
             dma((16,)), dma((16,)),

time: 74.7 us -> 64.5 us (0.86)
  Pallas kernels: 72.6 us -> 62.5 us
    pallas_call x1, Pallas kernels: 72.6 us -> 62.5 us  [body(): pl.pallas_call(call, out_shape=jax.ShapeDtypeStruct((128, 1024), f32), in...]
where the time goes in v2:
time: 64.5 us; the launch traced here: 64.4 us
  Pallas kernels  62.5 us (97%)
  local copies, waits for them, and re-layouts  1.89 us (3%)
    pallas_call x1, Pallas kernels, body(): pl.pallas_call(call, out_shape=jax.ShapeDtypeStruct((128, 1024), f32), in...  62.5 us
    unnamed x1, local copies, waits for them, and re-layouts  1.89 us

profile of v2, /device:TPU:1, one launch (start us, length us, event | category | flops | bytes accessed | tf_op | source)
XLA Modules:
  0.0 64.4 jit_solution(3163622804266258860)
XLA Ops:
  0.0 62.5 %influence.1 = f32[128,1024]{1,0:T(8,128)} custom-call(bf16[2048,896]{1,0:T(8,128)(2,1)} %refs_0_.1, bf16[2048,256]{1,0:T(8,128)(2,1)} %refs_1_.1, bf16[32,896]{1,0:T(8,128)(2,1)} %bitcast.2, bf16[32,256]{1,0:T(8,128)(2,1)} %bitcast.3, f32[64,1024]{1,0:T(8,128)} %refs_4_.1), custom_call_target="tpu_custom_call" | custom-call | tf_op jit(solution)/shard_map/influence/pallas_call | solution.py:423
  62.5 1.9 %copy.7 = f32[128,1024]{1,0:T(8,128)} copy(f32[128,1024]{1,0:T(8,128)} %influence.1) | data formatting | bytes 1048576

commit v3 on v2

--- a/solution.py
+++ b/solution.py
@@ -57,12 +57,23 @@
 def inverse(matrix):
     lane = iota((32, 128), 1)
     row_id = iota((32, 128), 0)
-    for k in range(32):
-        pivot = 1.0 / matrix[k : k + 1, k : k + 1]
-        row = jnp.where(lane[0:1] == k, 1.0, matrix[k : k + 1, :]) * pivot
-        column = jnp.where(row_id == k, -1.0, matrix[:, k : k + 1])
-        base = jnp.where((lane == k) | (row_id == k), 0.0, matrix)
-        matrix = base - column * row
+    for k in range(0, 32, 2):
+        row0, row1 = matrix[k : k + 1, :], matrix[k + 1 : k + 2, :]
+        first, cross = matrix[k : k + 1, k : k + 1], matrix[k : k + 1, k + 1 : k + 2]
+        last = matrix[k + 1 : k + 2, k + 1 : k + 2]
+        inv_first = 1.0 / first
+        ratio = cross * inv_first
+        inv_last = 1.0 / (last - cross * ratio)
+        top, side = inv_first + ratio * ratio * inv_last, -ratio * inv_last
+        at0, at1 = lane == k, lane == k + 1
+        down0, down1 = row_id == k, row_id == k + 1
+        row0 = jnp.where(at0[0:1], 1.0, jnp.where(at1[0:1], 0.0, row0))
+        row1 = jnp.where(at1[0:1], 1.0, jnp.where(at0[0:1], 0.0, row1))
+        column0 = jnp.where(down0, -1.0, jnp.where(down1, 0.0, matrix[:, k : k + 1]))
+        column1 = jnp.where(down1, -1.0, jnp.where(down0, 0.0, matrix[:, k + 1 : k + 2]))
+        base = jnp.where(at0 | at1 | down0 | down1, 0.0, matrix)
+        new0, new1 = top * row0 + side * row1, side * row0 + inv_last * row1
+        matrix = base - column0 * new0 - column1 * new1
     return matrix
 
 
@@ -128,15 +139,12 @@
 
     barrier = pltpu.get_barrier_semaphore()
 
-    def hello_z(i, carry):
-        pl.semaphore_signal(barrier, inc=1, device_id=(dp, at_z(i)), device_id_type=MESH)
-        return carry
-
     def hello_chip(i, carry):
         pl.semaphore_signal(barrier, inc=1, device_id=(chip(i), z), device_id_type=MESH)
         return carry
 
-    lax.fori_loop(1, 16, hello_z, 0)
+    for offset in (3, -3, 2, -2, 1, -1):
+        pl.semaphore_signal(barrier, inc=1, device_id=(dp, at_z(offset)), device_id_type=MESH)
     lax.fori_loop(1, 16, hello_chip, 0)
     pl.semaphore_signal(barrier, inc=1, device_id=(sibling, z), device_id_type=MESH)
 
@@ -159,7 +167,7 @@
     ).astype(bf16)
 
     own_q.wait()
-    pl.semaphore_wait(barrier, 31)
+    pl.semaphore_wait(barrier, 22)
 
     stage1 = []
     for m in (2, -2, 1, -1, 0):
@@ -180,11 +188,13 @@
             stage1.append(far)
     hub2r, hub2l, far_up, hub_2r, hub_2l, far_down, hub1r, hub1l, hub_1r, hub_1l, hub0r, hub0l = stage1
 
-    spread = []
-    for i, offset in enumerate((3, -3, 6, -6, 8)):
-        spread.append((remote(q_piece(z), q_piece(z), qz_send.at[i], qz_recv.at[i], (dp, at_z(offset))),
-                       remote(q_piece(z), q_piece(at_z(-offset)), qz_send.at[i], qz_recv.at[i], (dp, at_z(offset)))))
-        spread[-1][0].start()
+    def z_pass(i, offset, step):
+        held, coming = q_piece(at_z(offset)), q_piece(at_z(offset - step))
+        sems = (qz_send.at[i], qz_recv.at[i], (dp, at_z(step)))
+        remote(held, held, *sems).start()
+        return remote(held, coming, *sems)
+
+    spread = [z_pass(0, 0, 3), z_pass(1, 0, -3)]
 
     hub2r.wait_recv()
     hub2l.wait_recv()
@@ -200,6 +210,9 @@
     part[at_z(-6), 32:64, :] = part[at_z(-6), 32:64, :] + eighth[1]
     down2 = remote(part.at[at_z(-6)], second.at[1], rs_send.at[13], rs_recv.at[13], (dp, at_z(-3)))
     down2.start()
+    spread[0].wait()
+    spread[1].wait()
+    spread2 = [z_pass(2, -3, 3), z_pass(3, 3, -3)]
 
     hub1r.wait_recv()
     hub1l.wait_recv()
@@ -211,16 +224,6 @@
     hub0l.wait_recv()
     mine = part[z] + from_left[2] + from_right[2]
 
-    for pair in spread:
-        pair[1].wait()
-    near = []
-    for i, offset in enumerate((0, 3, -3, 6, -6)):
-        for side, base in ((1, 5), (-1, 10)):
-            held, coming = q_piece(at_z(offset)), q_piece(at_z(offset - side))
-            sems = (qz_send.at[base + i], qz_recv.at[base + i], (dp, at_z(side)))
-            near.append((remote(held, held, *sems), remote(held, coming, *sems)))
-            near[-1][0].start()
-
     up2.wait_recv()
     part[at_z(3)] = up + second[0]
     up3 = remote(part.at[at_z(3)], third.at[0], rs_send.at[14], rs_recv.at[14], (dp, at_z(3)))
@@ -229,6 +232,11 @@
     part[at_z(-3)] = down + second[1]
     down3 = remote(part.at[at_z(-3)], third.at[1], rs_send.at[15], rs_recv.at[15], (dp, at_z(-3)))
     down3.start()
+    spread2[0].wait()
+    spread2[1].wait()
+    near = [z_pass(4, 6, -2)]
+    for i, offset in enumerate((0, 3, -3, 6, -6)):
+        near += [z_pass(5 + i, offset, 1), z_pass(10 + i, offset, -1)]
 
     def plane(of_core, a, b):
         x, y = lax.rem(dp // 2, 4), dp // 8
@@ -274,8 +282,8 @@
         remote(q_block(which), q_block(which), qc_send.at[i], qc_recv.at[i], (sibling, z)).wait_recv()
         q_split(which)
 
-    for pair in near:
-        pair[1].wait()
+    for piece in near:
+        piece.wait()
     for da, db in ((1, 0), (-1, 0), (0, 1), (0, -1), (2, 0)):
         q_pass(0, 0, da, db)
     q_mate(0, 0)
@@ -334,9 +342,11 @@
     q_pass(1, -1, 0, 1)
     q_take(-1, 1)
     q_pass(-1, 1, 0, -1)
-    q_take(1, 1)
-    q_take(-1, -1)
-    for a, b in ((1, -1), (-1, 1), (1, 1), (-1, -1)):
+    q_take(2, 1)
+    q_pass(2, 1, 0, -1)
+    for a, b in ((1, 1), (-1, -1), (0, 2), (2, -1)):
+        q_take(a, b)
+    for a, b in ((1, -1), (-1, 1), (1, 1), (-1, -1), (2, 1), (0, 2), (2, -1)):
         q_split(plane(core, a, b))
     for a, b in ((1, 0), (-1, 0), (0, 1), (0, -1), (2, 0)):
         q_take_mate(a, b)
@@ -352,19 +362,11 @@
     swap = remote(minv, mpair, f_send.at[31], f_recv.at[31], (sibling, z))
     swap.start()
 
-    q_take(2, 1)
-    q_pass(2, 1, 0, -1)
-    q_take(2, -1)
-    q_take(0, 2)
-    q_take(1, 2)
-    q_take(-1, 2)
-    for a, b in ((2, 1), (2, -1), (0, 2), (1, 2), (-1, 2)):
+    for a, b in ((1, 2), (-1, 2), (2, 2)):
+        q_take(a, b)
         q_split(plane(core, a, b))
-    for a, b in ((1, -1), (-1, 1), (1, 1), (-1, -1), (2, 1), (2, -1), (0, 2), (1, 2), (-1, 2)):
+    for a, b in ((1, -1), (-1, 1), (1, 1), (-1, -1), (2, 1), (0, 2), (2, -1), (1, 2), (-1, 2), (2, 2)):
         q_take_mate(a, b)
-    q_take(2, 2)
-    q_split(plane(core, 2, 2))
-    q_take_mate(2, 2)
 
     swap.wait_recv()
     mine_inv, other_inv = minv[...], mpair[...]
@@ -422,7 +424,7 @@
 
     return pl.pallas_call(
         call,
-        out_shape=jax.ShapeDtypeStruct((128, 1024), f32),
+        out_shape=pltpu.VMEM((128, 1024), f32),
         in_specs=[hbm] * 5,
         out_specs=vmem,
         scratch_shapes=[
@@ -461,9 +463,12 @@
         ],
         name="influence",
         compiler_params=pltpu.CompilerParams(
-            collective_id=0, has_side_effects=True, vmem_limit_bytes=56 << 20
+            collective_id=0, has_side_effects=True, vmem_limit_bytes=24 << 20
         ),
-    )(hidden_acts, out_grads, proj_in.T, proj_out.T, query_codes)
+    )(*[
+        pltpu.with_memory_space_constraint(a, pltpu.HBM)
+        for a in (hidden_acts, out_grads, proj_in.T, proj_out.T, query_codes)
+    ])
 
 
 def solution(mesh):

time: 64.5 us -> 58.1 us (0.901)
  Pallas kernels: 62.5 us -> 57.2 us
  local copies, waits for them, and re-layouts: 1.89 us -> 0.8 us
    pallas_call x1, Pallas kernels: 62.5 us -> 57.2 us  [body(): pl.pallas_call(call, out_shape=pltpu.VMEM((128, 1024), f32), in_specs=[hb...]
    unnamed x1, local copies, waits for them, and re-layouts: 1.89 us -> 0.8 us
where the time goes in v3:
time: 58.1 us; the launch traced here: 58 us
  Pallas kernels  57.2 us (98%)
  local copies, waits for them, and re-layouts  0.8 us (1%)
    pallas_call x1, Pallas kernels, body(): pl.pallas_call(call, out_shape=pltpu.VMEM((128, 1024), f32), in_specs=[hb...  57.2 us

profile of v3, /device:TPU:1, one launch (start us, length us, event | category | flops | bytes accessed | tf_op | source)
XLA Modules:
  0.0 58.0 jit_solution(3105736377124775769)
XLA Ops:
  0.0 57.2 %influence.1 = f32[128,1024]{1,0:T(8,128)S(1)} custom-call(bf16[2048,896]{1,0:T(8,128)(2,1)} %refs_0_.1, bf16[2048,256]{1,0:T(8,128)(2,1)} %refs_1_.1, bf16[32,896]{1,0:T(8,128)(2,1)} %bitcast.2, bf16[32,256]{1,0:T(8,128)(2,1)} %bitcast.3, f32[64,1024]{1,0:T(8,128)} %refs_4_.1), custom_call_target="tpu_custom_call" | custom-call | tf_op jit(solution)/shard_map/influence/pallas_call | solution.py:425
  57.2 0.8 %copy.7 = f32[128,1024]{1,0:T(8,128)} copy(f32[128,1024]{1,0:T(8,128)S(1)} %influence.1) | data formatting | bytes 1048576

commit v4 on v3

--- a/solution.py
+++ b/solution.py
@@ -41,12 +41,20 @@
     return twice + pltpu.roll(twice, 64, 1)
 
 
-def pack(square):
-    lane = iota((8, 128), 1) // 32
-    tile = square[0:8]
-    for k in range(1, 4):
-        tile = jnp.where(lane == k, square[8 * k : 8 * k + 8], tile)
-    return tile
+def factors(product):
+    lane = iota((32, 128), 1) // 32
+
+    def block(k):
+        kept = jnp.where(lane == k, product[32 * k : 32 * k + 32], 0.0)
+        return pltpu.roll(kept, 128 - 32 * k, 1) if k else kept
+
+    def pack(square):
+        tile = square[0:8]
+        for k in range(1, 4):
+            tile = tile + pltpu.roll(square[8 * k : 8 * k + 8], 32 * k, 1)
+        return tile
+
+    return pack(block(0) + block(2)), pack(block(1) + block(3))
 
 
 def unpack(tile):
@@ -55,32 +63,39 @@
 
 
 def inverse(matrix):
-    lane = iota((32, 128), 1)
-    row_id = iota((32, 128), 0)
-    for k in range(0, 32, 2):
-        row0, row1 = matrix[k : k + 1, :], matrix[k + 1 : k + 2, :]
-        first, cross = matrix[k : k + 1, k : k + 1], matrix[k : k + 1, k + 1 : k + 2]
-        last = matrix[k + 1 : k + 2, k + 1 : k + 2]
-        inv_first = 1.0 / first
-        ratio = cross * inv_first
-        inv_last = 1.0 / (last - cross * ratio)
-        top, side = inv_first + ratio * ratio * inv_last, -ratio * inv_last
-        at0, at1 = lane == k, lane == k + 1
-        down0, down1 = row_id == k, row_id == k + 1
-        row0 = jnp.where(at0[0:1], 1.0, jnp.where(at1[0:1], 0.0, row0))
-        row1 = jnp.where(at1[0:1], 1.0, jnp.where(at0[0:1], 0.0, row1))
-        column0 = jnp.where(down0, -1.0, jnp.where(down1, 0.0, matrix[:, k : k + 1]))
-        column1 = jnp.where(down1, -1.0, jnp.where(down0, 0.0, matrix[:, k + 1 : k + 2]))
-        base = jnp.where(at0 | at1 | down0 | down1, 0.0, matrix)
-        new0, new1 = top * row0 + side * row1, side * row0 + inv_last * row1
-        matrix = base - column0 * new0 - column1 * new1
-    return matrix
+    lane = iota((1, 128), 1)
+    row_id = iota((8, 128), 0)
+    tiles = [matrix[8 * t : 8 * t + 8] for t in range(4)]
+    for b in range(4):
+        spread = [
+            [jnp.broadcast_to(tiles[t][:, 8 * b + j : 8 * b + j + 1], (8, 128)) for t in range(4)]
+            for j in range(8)
+        ]
+        for j in range(8):
+            k = 8 * b + j
+            columns = spread[j]
+            pivot = 1.0 / columns[b][j : j + 1]
+            row = jnp.where(lane == k, 1.0, tiles[b][j : j + 1]) * pivot
+            factors_next = [columns[b][n : n + 1] * pivot for n in range(j + 1, 8)]
+            columns = [jnp.where(row_id == j, -1.0, c) if t == b else c for t, c in enumerate(columns)]
+            for t in range(4):
+                kept = jnp.where(lane == k, 0.0, tiles[t])
+                if t == b:
+                    kept = jnp.where(row_id == j, 0.0, kept)
+                tiles[t] = kept - columns[t] * row
+            for n, factor in zip(range(j + 1, 8), factors_next):
+                for t in range(4):
+                    kept = spread[n][t]
+                    if t == b:
+                        kept = jnp.where(row_id == j, 0.0, kept)
+                    spread[n][t] = kept - columns[t] * factor
+    return jnp.concatenate(tiles, axis=0)
 
 
 def kernel(
     tokens, hid, grd, wi, wo, codes, out,
-    hbuf, gbuf, wip, wop, part, from_left, from_right, eighth, second, third,
-    fsend, fpair, ftile, fz, zsum, fp, minv, mpair, q, qhi, qlo, expand, chi, clo,
+    hbuf, gbuf, proj, part, from_left, from_right, eighth, second, third,
+    fsend, fpair, ftile, fz, zsum, fp, minv, mpair, q, qhi, qlo, expand, code_parts,
     weight_sem, load_sem, qload_sem, rs_send, rs_recv, f_send, f_recv,
     qz_send, qz_recv, qp_send, qp_recv, qc_send, qc_recv,
 ):
@@ -95,48 +110,15 @@
     def chip(i):
         return lax.rem(dp + 2 * i, 32)
 
+    def rel(offset):
+        return (offset - 5) % 16
+
     def remote(src, dst, ss, rs, device):
         return pltpu.make_async_remote_copy(
             src_ref=src, dst_ref=dst, send_sem=ss, recv_sem=rs,
             device_id=device, device_id_type=MESH,
         )
 
-    weights_in = []
-    for half in range(2):
-        for src, dst, at in ((wi, wip, 0), (wo, wop, 32)):
-            rows = pl.ds(64 * half + at, 32)
-            weights_in.append(pltpu.make_async_copy(
-                src, dst.at[half, rows, :], weight_sem.at[len(weights_in)]
-            ))
-    wip[...] = jnp.zeros_like(wip)
-    wop[...] = jnp.zeros_like(wop)
-    for copy in weights_in:
-        copy.start()
-    loads = []
-    for g in range(4):
-        rows = pl.ds(512 * g, 512)
-        loads.append((
-            pltpu.make_async_copy(hid.at[rows, :], hbuf.at[rows, :], load_sem.at[g, 0]),
-            pltpu.make_async_copy(grd.at[rows, :], gbuf.at[rows, :], load_sem.at[g, 1]),
-        ))
-        loads[-1][0].start()
-        loads[-1][1].start()
-
-    def q_rows(which):
-        return pl.ds(pl.multiple_of((which // 8) * 16, 16), 16)
-
-    def q_lanes(which):
-        return pl.ds(pl.multiple_of(lax.rem(which, 8) * 128, 128), 128)
-
-    def q_piece(from_z):
-        return q.at[from_z, q_rows(dp), q_lanes(dp)]
-
-    def q_block(which):
-        return q.at[:, q_rows(which), q_lanes(which)]
-
-    own_q = pltpu.make_async_copy(codes.at[q_rows(dp), q_lanes(dp)], q_piece(z), qload_sem)
-    own_q.start()
-
     barrier = pltpu.get_barrier_semaphore()
 
     def hello_chip(i, carry):
@@ -148,45 +130,82 @@
     lax.fori_loop(1, 16, hello_chip, 0)
     pl.semaphore_signal(barrier, inc=1, device_id=(sibling, z), device_id_type=MESH)
 
+    weights_in = []
+    for half in range(2):
+        for src, start, width, at in ((wi, 0, 896, 0), (wo, 896, 256, 32)):
+            rows = pl.ds(64 * half + at, 32)
+            lanes = pl.ds(1152 * half + start, width)
+            weights_in.append(pltpu.make_async_copy(
+                src, proj.at[rows, lanes], weight_sem.at[len(weights_in)]
+            ))
+    proj[...] = jnp.zeros_like(proj)
+    for copy in weights_in:
+        copy.start()
+    loads = []
+    chunks = ((0, 7), (7, 9))
+    for g, (start, count) in enumerate(chunks):
+        def load(j, carry, g=g):
+            rows = pl.ds(pl.multiple_of(at_z(5 + j) * 128, 128), 128)
+            pltpu.make_async_copy(hid.at[rows, :], hbuf.at[j], load_sem.at[g, 0]).start()
+            pltpu.make_async_copy(grd.at[rows, :], gbuf.at[j], load_sem.at[g, 1]).start()
+            return carry
+
+        lax.fori_loop(start, start + count, load, 0)
+        held = pl.ds(start, count)
+        loads.append((
+            pltpu.make_async_copy(hbuf.at[held], hbuf.at[held], load_sem.at[g, 0]),
+            pltpu.make_async_copy(gbuf.at[held], gbuf.at[held], load_sem.at[g, 1]),
+        ))
+
+    def q_rows(which):
+        return pl.ds(pl.multiple_of((which // 8) * 16, 16), 16)
+
+    def q_lanes(which):
+        return pl.ds(pl.multiple_of(lax.rem(which, 8) * 128, 128), 128)
+
+    def q_piece(from_z):
+        return q.at[from_z, q_rows(dp), q_lanes(dp)]
+
+    def q_block(which):
+        return q.at[:, q_rows(which), q_lanes(which)]
+
+    own_q = pltpu.make_async_copy(codes.at[q_rows(dp), q_lanes(dp)], q_piece(z), qload_sem)
+    own_q.start()
+
     for copy in weights_in:
         copy.wait()
-    for g in range(4):
+
+    def project(g):
+        start, count = chunks[g]
         loads[g][0].wait()
         loads[g][1].wait()
         total = None
         for half in range(2):
-            starts = [512 * g + 128 * j + 64 * half for j in range(4)]
-            h = jnp.concatenate([hbuf[s : s + 64, :] for s in starts], axis=0)
-            o = jnp.concatenate([gbuf[s : s + 64, :] for s in starts], axis=0)
-            term = dot_nt(h, wip[half]) + dot_nt(o, wop[half])
-            total = term if total is None else total + term
-        part[4 * g : 4 * g + 4] = total.reshape(4, 64, 128)
-
-    expand[...] = jnp.where(
-        iota((128, 1024), 1) // 32 == iota((128, 1024), 0), 1.0, 0.0
-    ).astype(bf16)
-
-    own_q.wait()
-    pl.semaphore_wait(barrier, 22)
+            rows = slice(64 * half, 64 * half + 64)
+            for ref, lane, width in ((hbuf, 0, 896), (gbuf, 896, 256)):
+                left = ref[start : start + count, rows, :].reshape(64 * count, width)
+                lane = lane + 1152 * half
+                term = dot_nt(left, proj[:, lane : lane + width])
+                total = term if total is None else total + term
+        part[start : start + count] = total.reshape(count, 64, 128)
 
     stage1 = []
-    for m in (2, -2, 1, -1, 0):
+
+    def to_hub(m):
         i = m + 2
-        right = remote(part.at[at_z(3 * m + 1)], from_left.at[i],
+        right = remote(part.at[rel(3 * m + 1)], from_left.at[i],
                        rs_send.at[i], rs_recv.at[i], (dp, at_z(1)))
-        left = remote(part.at[at_z(3 * m - 1)], from_right.at[i],
+        left = remote(part.at[rel(3 * m - 1)], from_right.at[i],
                       rs_send.at[5 + i], rs_recv.at[5 + i], (dp, at_z(-1)))
         right.start()
         left.start()
-        stage1 += [right, left]
+        stage1.extend([right, left])
         if abs(m) == 2:
             s = 0 if m == 2 else 1
-            far = remote(part.at[at_z(8), pl.ds(32 * s, 32), :], eighth.at[s],
-                         rs_send.at[10 + s], rs_recv.at[10 + s],
-                         (dp, at_z(2 if m == 2 else -2)))
+            far = remote(part.at[rel(8), pl.ds(32 * s, 32), :], eighth.at[s],
+                         rs_send.at[10 + s], rs_recv.at[10 + s], (dp, at_z(m)))
             far.start()
             stage1.append(far)
-    hub2r, hub2l, far_up, hub_2r, hub_2l, far_down, hub1r, hub1l, hub_1r, hub_1l, hub0r, hub0l = stage1
 
     def z_pass(i, offset, step):
         held, coming = q_piece(at_z(offset)), q_piece(at_z(offset - step))
@@ -194,49 +213,73 @@
         remote(held, held, *sems).start()
         return remote(held, coming, *sems)
 
+    project(0)
+    own_q.wait()
+    pl.semaphore_wait(barrier, 22)
+    to_hub(2)
+    to_hub(-2)
     spread = [z_pass(0, 0, 3), z_pass(1, 0, -3)]
+    project(1)
+    to_hub(1)
+    to_hub(-1)
+    to_hub(0)
+    hub2r, hub2l, far_up, hub_2r, hub_2l, far_down, hub1r, hub1l, hub_1r, hub_1l, hub0r, hub0l = stage1
+
+    spread[0].wait()
+    spread[1].wait()
+    spread2 = [z_pass(2, -3, 3), z_pass(3, 3, -3)]
+
+    halves = (slice(0, 32), slice(32, 64))
+
+    def half_pass(i, src, dst, half, step):
+        copy = remote(src.at[pl.ds(32 * half, 32), :], dst.at[pl.ds(32 * half, 32), :],
+                      rs_send.at[i], rs_recv.at[i], (dp, at_z(step)))
+        copy.start()
+        return copy
 
     hub2r.wait_recv()
     hub2l.wait_recv()
     far_up.wait_recv()
-    part[at_z(6)] = part[at_z(6)] + from_left[4] + from_right[4]
-    part[at_z(6), 0:32, :] = part[at_z(6), 0:32, :] + eighth[0]
-    up2 = remote(part.at[at_z(6)], second.at[0], rs_send.at[12], rs_recv.at[12], (dp, at_z(3)))
-    up2.start()
+    part[rel(6)] = part[rel(6)] + from_left[4] + from_right[4]
+    part[rel(6), 0:32, :] = part[rel(6), 0:32, :] + eighth[0]
+    up2 = [half_pass(12, part.at[rel(6)], second.at[0], 0, 3)]
     hub_2r.wait_recv()
     hub_2l.wait_recv()
     far_down.wait_recv()
-    part[at_z(-6)] = part[at_z(-6)] + from_left[0] + from_right[0]
-    part[at_z(-6), 32:64, :] = part[at_z(-6), 32:64, :] + eighth[1]
-    down2 = remote(part.at[at_z(-6)], second.at[1], rs_send.at[13], rs_recv.at[13], (dp, at_z(-3)))
-    down2.start()
-    spread[0].wait()
-    spread[1].wait()
-    spread2 = [z_pass(2, -3, 3), z_pass(3, 3, -3)]
+    part[rel(-6)] = part[rel(-6)] + from_left[0] + from_right[0]
+    part[rel(-6), 32:64, :] = part[rel(-6), 32:64, :] + eighth[1]
+    down2 = [half_pass(13, part.at[rel(-6)], second.at[1], 0, -3)]
+    up2.append(half_pass(14, part.at[rel(6)], second.at[0], 1, 3))
+    down2.append(half_pass(15, part.at[rel(-6)], second.at[1], 1, -3))
 
     hub1r.wait_recv()
     hub1l.wait_recv()
     hub_1r.wait_recv()
     hub_1l.wait_recv()
-    up = part[at_z(3)] + from_left[3] + from_right[3]
-    down = part[at_z(-3)] + from_left[1] + from_right[1]
+    up = part[rel(3)] + from_left[3] + from_right[3]
+    down = part[rel(-3)] + from_left[1] + from_right[1]
     hub0r.wait_recv()
     hub0l.wait_recv()
-    mine = part[z] + from_left[2] + from_right[2]
-
-    up2.wait_recv()
-    part[at_z(3)] = up + second[0]
-    up3 = remote(part.at[at_z(3)], third.at[0], rs_send.at[14], rs_recv.at[14], (dp, at_z(3)))
-    up3.start()
-    down2.wait_recv()
-    part[at_z(-3)] = down + second[1]
-    down3 = remote(part.at[at_z(-3)], third.at[1], rs_send.at[15], rs_recv.at[15], (dp, at_z(-3)))
-    down3.start()
+    mine = part[rel(0)] + from_left[2] + from_right[2]
+
+    expand[...] = jnp.where(
+        iota((128, 1024), 1) // 32 == iota((128, 1024), 0), 1.0, 0.0
+    ).astype(bf16)
+
     spread2[0].wait()
     spread2[1].wait()
     near = [z_pass(4, 6, -2)]
     for i, offset in enumerate((0, 3, -3, 6, -6)):
         near += [z_pass(5 + i, offset, 1), z_pass(10 + i, offset, -1)]
+
+    up3, down3 = [], []
+    for h, rows in enumerate(halves):
+        up2[h].wait_recv()
+        part[rel(3), rows, :] = up[rows] + second[0, rows, :]
+        up3.append(half_pass(16 + h, part.at[rel(3)], third.at[0], h, 3))
+        down2[h].wait_recv()
+        part[rel(-3), rows, :] = down[rows] + second[1, rows, :]
+        down3.append(half_pass(18 + h, part.at[rel(-3)], third.at[1], h, -3))
 
     def plane(of_core, a, b):
         x, y = lax.rem(dp // 2, 4), dp // 8
@@ -289,14 +332,11 @@
     q_mate(0, 0)
     q_split(dp)
 
-    up3.wait_recv()
-    down3.wait_recv()
+    for copy in up3 + down3:
+        copy.wait_recv()
     x = mine + third[0] + third[1]
 
-    acts4 = jnp.concatenate([tile_lanes(x, 0), tile_lanes(x, 64)], axis=0)
-    grads4 = jnp.concatenate([tile_lanes(x, 32), tile_lanes(x, 96)], axis=0)
-    fin = pack(dot_tn(acts4, acts4, HIGHEST)[0:32])
-    fout = pack(dot_tn(grads4, grads4, HIGHEST)[0:32])
+    fin, fout = factors(dot_tn(x, x, HIGHEST))
     first_core = core == 0
     fsend[...] = jnp.where(first_core, fout, fin)
     fisher_pair = remote(fsend, fpair, f_send.at[0], f_recv.at[0], (sibling, z))
@@ -389,20 +429,21 @@
         wide = dot_nn(grads_high, expand[:, lanes]) + dot_nn(grads_low, expand[:, lanes])
         code = wide * acts_ready
         high = code.astype(bf16)
-        chi[:, lanes] = high
-        clo[:, lanes] = (code - high.astype(f32)).astype(bf16)
+        code_parts[0:128, lanes] = high
+        code_parts[128:256, lanes] = (code - high.astype(f32)).astype(bf16)
 
     def score(i, carry):
         rows = pl.ds(pl.multiple_of(i * 256, 256), 256)
         four = pl.ds(4 * i, 4)
         high = qhi[four].reshape(256, 1024)
         low = qlo[four].reshape(256, 1024)
-        out[:, rows] = dot_nt(chi[...], high) + dot_nt(clo[...], high) + dot_nt(chi[...], low)
+        by_high = dot_nt(code_parts[...], high)
+        out[:, rows] = by_high[0:128] + by_high[128:256] + dot_nt(code_parts[0:128, :], low)
         return carry
 
     lax.fori_loop(0, 4, score, 0)
 
-    for copy in stage1 + [up2, down2, up3, down3, fisher_pair, swap] + q_sent:
+    for copy in stage1 + up2 + down2 + up3 + down3 + [fisher_pair, swap] + q_sent:
         copy.wait_send()
 
     def sent(i, carry):
@@ -428,10 +469,9 @@
         in_specs=[hbm] * 5,
         out_specs=vmem,
         scratch_shapes=[
-            pltpu.VMEM((2048, 896), bf16),
-            pltpu.VMEM((2048, 256), bf16),
-            pltpu.VMEM((2, 128, 896), bf16),
-            pltpu.VMEM((2, 128, 256), bf16),
+            pltpu.VMEM((16, 128, 896), bf16),
+            pltpu.VMEM((16, 128, 256), bf16),
+            pltpu.VMEM((128, 2304), bf16),
             pltpu.VMEM((16, 64, 128), f32),
             pltpu.VMEM((5, 64, 128), f32),
             pltpu.VMEM((5, 64, 128), f32),
@@ -450,12 +490,11 @@
             pltpu.VMEM((16, 64, 1024), bf16),
             pltpu.VMEM((16, 64, 1024), bf16),
             pltpu.VMEM((128, 1024), bf16),
-            pltpu.VMEM((128, 1024), bf16),
-            pltpu.VMEM((128, 1024), bf16),
+            pltpu.VMEM((256, 1024), bf16),
             dma((4,)),
-            dma((4, 2)),
+            dma((2, 2)),
             dma,
-            dma((16,)), dma((16,)),
+            dma((20,)), dma((20,)),
             dma((32,)), dma((32,)),
             dma((16,)), dma((16,)),
             dma((16,)), dma((16,)),

time: 58.1 us -> 52 us (0.90)
  Pallas kernels: 57.2 us -> 51.1 us
    pallas_call x1, Pallas kernels: 57.2 us -> 51.1 us  [body(): pl.pallas_call(call, out_shape=pltpu.VMEM((128, 1024), f32), in_specs=[hb...]
where the time goes in v4:
time: 52 us; the launch traced here: 51.9 us
  Pallas kernels  51.1 us (98%)
  local copies, waits for them, and re-layouts  0.8 us (2%)
    pallas_call x1, Pallas kernels, body(): pl.pallas_call(call, out_shape=pltpu.VMEM((128, 1024), f32), in_specs=[hb...  51.1 us

profile of v4, /device:TPU:1, one launch (start us, length us, event | category | flops | bytes accessed | tf_op | source)
XLA Modules:
  0.0 51.9 jit_solution(9063933422302277455)
XLA Ops:
  0.0 51.1 %influence.1 = f32[128,1024]{1,0:T(8,128)S(1)} custom-call(bf16[2048,896]{1,0:T(8,128)(2,1)} %refs_0_.1, bf16[2048,256]{1,0:T(8,128)(2,1)} %refs_1_.1, bf16[32,896]{1,0:T(8,128)(2,1)} %bitcast.2, bf16[32,256]{1,0:T(8,128)(2,1)} %bitcast.3, f32[64,1024]{1,0:T(8,128)} %refs_4_.1), custom_call_target="tpu_custom_call" | custom-call | tf_op jit(solution)/shard_map/influence/pallas_call | solution.py:466
  51.1 0.8 %copy.7 = f32[128,1024]{1,0:T(8,128)} copy(f32[128,1024]{1,0:T(8,128)S(1)} %influence.1) | data formatting | bytes 1048576

commit v5 on v4

--- a/solution.py
+++ b/solution.py
@@ -32,13 +32,6 @@
 
 def iota(shape, axis):
     return lax.broadcasted_iota(jnp.int32, shape, axis)
-
-
-def tile_lanes(x, start):
-    lane = iota(x.shape, 1)
-    kept = jnp.where((lane >= start) & (lane < start + 32), x, 0.0)
-    twice = kept + pltpu.roll(kept, 32, 1)
-    return twice + pltpu.roll(twice, 64, 1)
 
 
 def factors(product):
@@ -95,8 +88,8 @@
 def kernel(
     tokens, hid, grd, wi, wo, codes, out,
     hbuf, gbuf, proj, part, from_left, from_right, eighth, second, third,
-    fsend, fpair, ftile, fz, zsum, fp, minv, mpair, q, qhi, qlo, expand, code_parts,
-    weight_sem, load_sem, qload_sem, rs_send, rs_recv, f_send, f_recv,
+    fsend, fpair, ftile, fz, zsum, fp, minv, mpair, q, qhi, qlo, code_parts,
+    weight_sem, load_sem, qload_sem, rs_send, rs_recv, f_send, f_recv, fsum_send, fsum_recv,
     qz_send, qz_recv, qp_send, qp_recv, qc_send, qc_recv,
 ):
     dp = lax.axis_index("dp")
@@ -216,9 +209,9 @@
     project(0)
     own_q.wait()
     pl.semaphore_wait(barrier, 22)
+    spread = [z_pass(0, 0, 3), z_pass(1, 0, -3)]
     to_hub(2)
     to_hub(-2)
-    spread = [z_pass(0, 0, 3), z_pass(1, 0, -3)]
     project(1)
     to_hub(1)
     to_hub(-1)
@@ -262,10 +255,6 @@
     hub0l.wait_recv()
     mine = part[rel(0)] + from_left[2] + from_right[2]
 
-    expand[...] = jnp.where(
-        iota((128, 1024), 1) // 32 == iota((128, 1024), 0), 1.0, 0.0
-    ).astype(bf16)
-
     spread2[0].wait()
     spread2[1].wait()
     near = [z_pass(4, 6, -2)]
@@ -327,7 +316,7 @@
 
     for piece in near:
         piece.wait()
-    for da, db in ((1, 0), (-1, 0), (0, 1), (0, -1), (2, 0)):
+    for da, db in ((1, 0), (-1, 0), (2, 0), (0, 1), (0, -1)):
         q_pass(0, 0, da, db)
     q_mate(0, 0)
     q_split(dp)
@@ -345,113 +334,97 @@
     fisher_pair.wait_recv()
     ftile[...] = keep + fpair[...]
 
-    def send_fz(i, carry):
-        j = lax.rem(i + 7, 15) + 1
-        remote(ftile, fz.at[j], f_send.at[j], f_recv.at[j], (dp, at_z(j))).start()
-        return carry
-
-    lax.fori_loop(0, 15, send_fz, 0)
-
-    for a in (1, -1):
+    others = pl.ds(1, 15)
+    for i in (8, 7, 9, 6, 10, 5, 11, 4, 12, 3, 13, 2, 14, 1, 15):
+        remote(ftile, fz.at[i], fsum_send.at[0], fsum_recv.at[0], (dp, at_z(i))).start()
+
+    turned = x.T
+    acts_turned = jnp.concatenate([turned[0:32], turned[64:96]], axis=1)
+    grads_turned = jnp.concatenate([turned[32:64], turned[96:128]], axis=1)
+
+    for a in (1, -1, 2):
         q_take(a, 0)
         q_pass(a, 0, 0, 1)
         q_pass(a, 0, 0, -1)
+    q_pass(2, 0, 0, 2)
+    q_take(0, 1)
+    q_pass(0, 1, 0, -1)
     q_take(0, -1)
-    q_pass(0, -1, 0, 1)
-    q_take(0, 1)
-    q_take(2, 0)
-    q_pass(2, 0, 0, 1)
-    q_pass(2, 0, 0, -1)
     for a, b in ((1, 0), (-1, 0), (0, 1), (0, -1), (2, 0)):
         q_split(plane(core, a, b))
     q_take_mate(0, 0)
 
-    def wait_fz(i, total):
-        remote(ftile, fz.at[i], f_send.at[i], f_recv.at[i], (dp, at_z(i))).wait_recv()
-        return total + fz[i]
-
-    zsum[...] = lax.fori_loop(1, 16, wait_fz, ftile[...])
-
-    def send_fp(i, carry):
-        remote(zsum, fp.at[i], f_send.at[15 + i], f_recv.at[15 + i], (chip(i), z)).start()
-        return carry
-
-    lax.fori_loop(1, 16, send_fp, 0)
-
-    q_take(1, -1)
-    q_pass(1, -1, 0, 1)
-    q_take(-1, 1)
-    q_pass(-1, 1, 0, -1)
-    q_take(2, 1)
-    q_pass(2, 1, 0, -1)
-    for a, b in ((1, 1), (-1, -1), (0, 2), (2, -1)):
+    def take_all(own, ref, which):
+        pltpu.make_async_copy(ref.at[others], ref.at[others], fsum_recv.at[which]).wait()
+        terms = [own[...]] + [ref[i] for i in range(1, 16)]
+        while len(terms) > 1:
+            terms = [a + b for a, b in zip(terms[::2], terms[1::2])]
+        return terms[0]
+
+    zsum[...] = take_all(ftile, fz, 0)
+    for i in (10, 6, 9, 11, 5, 7, 2, 14, 8, 4, 12, 3, 13, 1, 15):
+        remote(zsum, fp.at[i], fsum_send.at[1], fsum_recv.at[1], (chip(i), z)).start()
+
+    def sent_all(ref, which):
+        pltpu.make_async_copy(ref.at[others], ref.at[others], fsum_send.at[which]).wait()
+
+    for copy in stage1 + up2 + down2 + up3 + down3 + [fisher_pair]:
+        copy.wait_send()
+    sent_all(fz, 0)
+
+    for a in (1, -1):
+        q_take(a, 1)
+        q_pass(a, 1, 0, -1)
+    for a, b in ((1, -1), (-1, -1), (0, 2), (2, 1), (2, -1)):
         q_take(a, b)
-    for a, b in ((1, -1), (-1, 1), (1, 1), (-1, -1), (2, 1), (0, 2), (2, -1)):
+    for a, b in ((1, 1), (-1, 1), (1, -1), (-1, -1), (0, 2), (2, 1), (2, -1)):
         q_split(plane(core, a, b))
-    for a, b in ((1, 0), (-1, 0), (0, 1), (0, -1), (2, 0)):
+    for a, b in ((1, 0), (-1, 0), (0, 1), (0, -1), (2, 0), (1, 1), (-1, 1), (1, -1), (-1, -1), (0, 2)):
         q_take_mate(a, b)
 
-    def wait_fp(i, total):
-        remote(zsum, fp.at[i], f_send.at[15 + i], f_recv.at[15 + i], (chip(i), z)).wait_recv()
-        return total + fp[i]
-
-    fisher = unpack(lax.fori_loop(1, 16, wait_fp, zsum[...]))
+    for copy in q_sent[:6]:
+        copy.wait_send()
+    fisher = unpack(take_all(zsum, fp, 1))
     eye = iota((32, 128), 0) == iota((32, 128), 1)
     fisher = fisher / tokens + jnp.where(eye, damping, 0.0)
     minv[...] = inverse(jnp.where(iota((32, 128), 1) < 32, fisher, 0.0))
-    swap = remote(minv, mpair, f_send.at[31], f_recv.at[31], (sibling, z))
+    swap = remote(minv, mpair, f_send.at[1], f_recv.at[1], (sibling, z))
     swap.start()
 
-    for a, b in ((1, 2), (-1, 2), (2, 2)):
+    for a, b in ((2, 2), (1, 2), (-1, 2)):
         q_take(a, b)
         q_split(plane(core, a, b))
-    for a, b in ((1, -1), (-1, 1), (1, 1), (-1, -1), (2, 1), (0, 2), (2, -1), (1, 2), (-1, 2), (2, 2)):
+    for a, b in ((2, 1), (2, -1), (2, 2), (1, 2), (-1, 2)):
         q_take_mate(a, b)
 
     swap.wait_recv()
     mine_inv, other_inv = minv[...], mpair[...]
-    inv_in = tile_lanes(jnp.where(first_core, mine_inv, other_inv), 0)
-    inv_out = jnp.where(first_core, other_inv, mine_inv)
-    zero = jnp.zeros((32, 128), f32)
-    weights = jnp.concatenate([
-        jnp.concatenate([inv_in, zero, zero, zero], axis=0),
-        jnp.concatenate([zero, zero, inv_in, zero], axis=0),
-        jnp.concatenate([zero, inv_out, zero, zero], axis=0),
-        jnp.concatenate([zero, zero, zero, inv_out], axis=0),
-    ], axis=1)
-    ready = dot_nn(x, weights, HIGHEST)
-    acts_ready = jnp.concatenate([ready[:, 0:128], ready[:, 128:256]], axis=0)
-    grads_ready = jnp.concatenate([ready[:, 256:384], ready[:, 384:512]], axis=0) * (1.0 / 32.0)
-    grads_high = grads_ready.astype(bf16)
-    grads_low = (grads_ready - grads_high.astype(f32)).astype(bf16)
-    for k in range(8):
-        lanes = slice(128 * k, 128 * k + 128)
-        wide = dot_nn(grads_high, expand[:, lanes]) + dot_nn(grads_low, expand[:, lanes])
-        code = wide * acts_ready
+    inv_in = jnp.where(first_core, mine_inv, other_inv)[:, 0:32]
+    inv_out = jnp.where(first_core, other_inv, mine_inv)[:, 0:32]
+    acts_ready = dot_nn(inv_in, acts_turned, HIGHEST)
+    grads_ready = dot_nn(inv_out, grads_turned, HIGHEST) * (1.0 / 32.0)
+    for a in range(32):
+        rows = slice(32 * a, 32 * a + 32)
+        code = grads_ready[a : a + 1] * acts_ready
         high = code.astype(bf16)
-        code_parts[0:128, lanes] = high
-        code_parts[128:256, lanes] = (code - high.astype(f32)).astype(bf16)
+        code_parts[rows, 0:128] = high
+        code_parts[rows, 128:256] = (code - high.astype(f32)).astype(bf16)
 
     def score(i, carry):
         rows = pl.ds(pl.multiple_of(i * 256, 256), 256)
         four = pl.ds(4 * i, 4)
         high = qhi[four].reshape(256, 1024)
         low = qlo[four].reshape(256, 1024)
-        by_high = dot_nt(code_parts[...], high)
-        out[:, rows] = by_high[0:128] + by_high[128:256] + dot_nt(code_parts[0:128, :], low)
+        by_high = dot_nn(high, code_parts[...])
+        by_low = dot_nn(low, code_parts[:, 0:128])
+        out[:, rows] = (by_high[:, 0:128] + by_high[:, 128:256] + by_low).T
         return carry
 
     lax.fori_loop(0, 4, score, 0)
 
-    for copy in stage1 + up2 + down2 + up3 + down3 + [fisher_pair, swap] + q_sent:
+    for copy in [swap] + q_sent[6:]:
         copy.wait_send()
-
-    def sent(i, carry):
-        remote(ftile, fz.at[i], f_send.at[i], f_recv.at[i], (dp, at_z(i))).wait_send()
-        remote(zsum, fp.at[i], f_send.at[15 + i], f_recv.at[15 + i], (chip(i), z)).wait_send()
-        return carry
-
-    lax.fori_loop(1, 16, sent, 0)
+    sent_all(fp, 1)
 
 
 def body(hidden_acts, out_grads, proj_in, proj_out, query_codes):
@@ -489,13 +462,13 @@
             pltpu.VMEM((16, 64, 1024), f32),
             pltpu.VMEM((16, 64, 1024), bf16),
             pltpu.VMEM((16, 64, 1024), bf16),
-            pltpu.VMEM((128, 1024), bf16),
-            pltpu.VMEM((256, 1024), bf16),
+            pltpu.VMEM((1024, 256), bf16),
             dma((4,)),
             dma((2, 2)),
             dma,
             dma((20,)), dma((20,)),
-            dma((32,)), dma((32,)),
+            dma((2,)), dma((2,)),
+            dma((2,)), dma((2,)),
             dma((16,)), dma((16,)),
             dma((16,)), dma((16,)),
             dma((16,)), dma((16,)),

time: 52 us -> 50.2 us (0.965)
  Pallas kernels: 51.1 us -> 49.3 us
    pallas_call x1, Pallas kernels: 51.1 us -> 49.3 us  [body(): pl.pallas_call(call, out_shape=pltpu.VMEM((128, 1024), f32), in_specs=[hb...]
where the time goes in v5:
time: 50.2 us; the launch traced here: 50.1 us
  Pallas kernels  49.3 us (98%)
  local copies, waits for them, and re-layouts  0.8 us (2%)
    pallas_call x1, Pallas kernels, body(): pl.pallas_call(call, out_shape=pltpu.VMEM((128, 1024), f32), in_specs=[hb...  49.3 us

profile of v5, /device:TPU:1, one launch (start us, length us, event | category | flops | bytes accessed | tf_op | source)
XLA Modules:
  0.0 50.1 jit_solution(11810678765367095775)
XLA Ops:
  0.0 49.3 %influence.1 = f32[128,1024]{1,0:T(8,128)S(1)} custom-call(bf16[2048,896]{1,0:T(8,128)(2,1)} %refs_0_.1, bf16[2048,256]{1,0:T(8,128)(2,1)} %refs_1_.1, bf16[32,896]{1,0:T(8,128)(2,1)} %bitcast.2, bf16[32,256]{1,0:T(8,128)(2,1)} %bitcast.3, f32[64,1024]{1,0:T(8,128)} %refs_4_.1), custom_call_target="tpu_custom_call" | custom-call | tf_op jit(solution)/shard_map/influence/pallas_call | solution.py:439
  49.3 0.8 %copy.7 = f32[128,1024]{1,0:T(8,128)} copy(f32[128,1024]{1,0:T(8,128)S(1)} %influence.1) | data formatting | bytes 1048576

commit v6 on v5

--- a/solution.py
+++ b/solution.py
@@ -87,7 +87,7 @@
 
 def kernel(
     tokens, hid, grd, wi, wo, codes, out,
-    hbuf, gbuf, proj, part, from_left, from_right, eighth, second, third,
+    hbuf, gbuf, proj, part, inbox, second, third,
     fsend, fpair, ftile, fz, zsum, fp, minv, mpair, q, qhi, qlo, code_parts,
     weight_sem, load_sem, qload_sem, rs_send, rs_recv, f_send, f_recv, fsum_send, fsum_recv,
     qz_send, qz_recv, qp_send, qp_recv, qc_send, qc_recv,
@@ -123,13 +123,16 @@
     lax.fori_loop(1, 16, hello_chip, 0)
     pl.semaphore_signal(barrier, inc=1, device_id=(sibling, z), device_id_type=MESH)
 
+    def wait_bytes(ref, sem):
+        pltpu.make_async_copy(ref, ref, sem).wait()
+
     weights_in = []
     for half in range(2):
         for src, start, width, at in ((wi, 0, 896, 0), (wo, 896, 256, 32)):
             rows = pl.ds(64 * half + at, 32)
             lanes = pl.ds(1152 * half + start, width)
             weights_in.append(pltpu.make_async_copy(
-                src, proj.at[rows, lanes], weight_sem.at[len(weights_in)]
+                src, proj.at[rows, lanes], weight_sem
             ))
     proj[...] = jnp.zeros_like(proj)
     for copy in weights_in:
@@ -165,8 +168,7 @@
     own_q = pltpu.make_async_copy(codes.at[q_rows(dp), q_lanes(dp)], q_piece(z), qload_sem)
     own_q.start()
 
-    for copy in weights_in:
-        copy.wait()
+    wait_bytes(proj.at[pl.ds(0, 64), pl.ds(0, 1152)], weight_sem)
 
     def project(g):
         start, count = chunks[g]
@@ -182,93 +184,77 @@
                 total = term if total is None else total + term
         part[start : start + count] = total.reshape(count, 64, 128)
 
-    stage1 = []
-
     def to_hub(m):
         i = m + 2
-        right = remote(part.at[rel(3 * m + 1)], from_left.at[i],
-                       rs_send.at[i], rs_recv.at[i], (dp, at_z(1)))
-        left = remote(part.at[rel(3 * m - 1)], from_right.at[i],
-                      rs_send.at[5 + i], rs_recv.at[5 + i], (dp, at_z(-1)))
-        right.start()
-        left.start()
-        stage1.extend([right, left])
+        remote(part.at[rel(3 * m + 1)], inbox.at[i, pl.ds(0, 64)],
+               rs_send, rs_recv.at[i], (dp, at_z(1))).start()
+        remote(part.at[rel(3 * m - 1)], inbox.at[i, pl.ds(64, 64)],
+               rs_send, rs_recv.at[i], (dp, at_z(-1))).start()
         if abs(m) == 2:
-            s = 0 if m == 2 else 1
-            far = remote(part.at[rel(8), pl.ds(32 * s, 32), :], eighth.at[s],
-                         rs_send.at[10 + s], rs_recv.at[10 + s], (dp, at_z(m)))
-            far.start()
-            stage1.append(far)
+            s = 0 if m == 2 else 32
+            remote(part.at[rel(8), pl.ds(s, 32), :], inbox.at[i, pl.ds(128, 32)],
+                   rs_send, rs_recv.at[i], (dp, at_z(m))).start()
+
+    def hub(m):
+        i = m + 2
+        wait_bytes(inbox.at[i, pl.ds(0, 160 if abs(m) == 2 else 128)], rs_recv.at[i])
+        return part[rel(3 * m)] + inbox[i, 0:64, :] + inbox[i, 64:128, :]
 
     def z_pass(i, offset, step):
-        held, coming = q_piece(at_z(offset)), q_piece(at_z(offset - step))
-        sems = (qz_send.at[i], qz_recv.at[i], (dp, at_z(step)))
-        remote(held, held, *sems).start()
-        return remote(held, coming, *sems)
+        held = q_piece(at_z(offset))
+        remote(held, held, qz_send, qz_recv.at[i], (dp, at_z(step))).start()
+
+    def z_wait(i, pieces):
+        wait_bytes(q.at[pl.ds(0, pieces), pl.ds(0, 16), pl.ds(0, 128)], qz_recv.at[i])
 
     project(0)
     own_q.wait()
     pl.semaphore_wait(barrier, 22)
-    spread = [z_pass(0, 0, 3), z_pass(1, 0, -3)]
+    z_pass(0, 0, 3)
+    z_pass(0, 0, -3)
     to_hub(2)
     to_hub(-2)
     project(1)
     to_hub(1)
     to_hub(-1)
     to_hub(0)
-    hub2r, hub2l, far_up, hub_2r, hub_2l, far_down, hub1r, hub1l, hub_1r, hub_1l, hub0r, hub0l = stage1
-
-    spread[0].wait()
-    spread[1].wait()
-    spread2 = [z_pass(2, -3, 3), z_pass(3, 3, -3)]
+
+    z_wait(0, 2)
+    z_pass(1, -3, 3)
+    z_pass(1, 3, -3)
 
     halves = (slice(0, 32), slice(32, 64))
 
     def half_pass(i, src, dst, half, step):
         copy = remote(src.at[pl.ds(32 * half, 32), :], dst.at[pl.ds(32 * half, 32), :],
-                      rs_send.at[i], rs_recv.at[i], (dp, at_z(step)))
+                      rs_send, rs_recv.at[i], (dp, at_z(step)))
         copy.start()
         return copy
 
-    hub2r.wait_recv()
-    hub2l.wait_recv()
-    far_up.wait_recv()
-    part[rel(6)] = part[rel(6)] + from_left[4] + from_right[4]
-    part[rel(6), 0:32, :] = part[rel(6), 0:32, :] + eighth[0]
-    up2 = [half_pass(12, part.at[rel(6)], second.at[0], 0, 3)]
-    hub_2r.wait_recv()
-    hub_2l.wait_recv()
-    far_down.wait_recv()
-    part[rel(-6)] = part[rel(-6)] + from_left[0] + from_right[0]
-    part[rel(-6), 32:64, :] = part[rel(-6), 32:64, :] + eighth[1]
-    down2 = [half_pass(13, part.at[rel(-6)], second.at[1], 0, -3)]
-    up2.append(half_pass(14, part.at[rel(6)], second.at[0], 1, 3))
-    down2.append(half_pass(15, part.at[rel(-6)], second.at[1], 1, -3))
-
-    hub1r.wait_recv()
-    hub1l.wait_recv()
-    hub_1r.wait_recv()
-    hub_1l.wait_recv()
-    up = part[rel(3)] + from_left[3] + from_right[3]
-    down = part[rel(-3)] + from_left[1] + from_right[1]
-    hub0r.wait_recv()
-    hub0l.wait_recv()
-    mine = part[rel(0)] + from_left[2] + from_right[2]
-
-    spread2[0].wait()
-    spread2[1].wait()
-    near = [z_pass(4, 6, -2)]
-    for i, offset in enumerate((0, 3, -3, 6, -6)):
-        near += [z_pass(5 + i, offset, 1), z_pass(10 + i, offset, -1)]
-
-    up3, down3 = [], []
+    part[rel(6)] = hub(2)
+    part[rel(6), 0:32, :] = part[rel(6), 0:32, :] + inbox[4, 128:160, :]
+    up2 = [half_pass(5, part.at[rel(6)], second.at[0], 0, 3)]
+    part[rel(-6)] = hub(-2)
+    part[rel(-6), 32:64, :] = part[rel(-6), 32:64, :] + inbox[0, 128:160, :]
+    down2 = [half_pass(6, part.at[rel(-6)], second.at[1], 0, -3)]
+    up2.append(half_pass(7, part.at[rel(6)], second.at[0], 1, 3))
+    down2.append(half_pass(8, part.at[rel(-6)], second.at[1], 1, -3))
+
+    up, down, mine = hub(1), hub(-1), hub(0)
+
+    z_wait(1, 2)
+    z_pass(2, 6, -2)
+    for offset in (0, 3, -3, 6, -6):
+        z_pass(2, offset, 1)
+        z_pass(2, offset, -1)
+
     for h, rows in enumerate(halves):
         up2[h].wait_recv()
         part[rel(3), rows, :] = up[rows] + second[0, rows, :]
-        up3.append(half_pass(16 + h, part.at[rel(3)], third.at[0], h, 3))
+        half_pass(9, part.at[rel(3)], third.at[0], h, 3)
         down2[h].wait_recv()
         part[rel(-3), rows, :] = down[rows] + second[1, rows, :]
-        down3.append(half_pass(18 + h, part.at[rel(-3)], third.at[1], h, -3))
+        half_pass(9, part.at[rel(-3)], third.at[1], h, -3)
 
     def plane(of_core, a, b):
         x, y = lax.rem(dp // 2, 4), dp // 8
@@ -279,14 +265,18 @@
     def index(a, b):
         return 4 * (a % 4) + b % 4
 
-    q_sent = []
+    groups = (
+        ((0, 0),),
+        ((1, 0), (-1, 0), (0, 1), (0, -1), (2, 0)),
+        ((1, 1), (-1, 1), (1, -1), (-1, -1), (0, 2)),
+        ((2, 1), (2, -1), (2, 2), (1, 2), (-1, 2)),
+    )
+    group = {place: g for g, places in enumerate(groups) for place in places}
 
     def q_pass(a, b, da, db):
         i = index(a - da, b - db)
         block = q_block(plane(core, a, b))
-        copy = remote(block, block, qp_send.at[i], qp_recv.at[i], (plane(core, da, db), z))
-        copy.start()
-        q_sent.append(copy)
+        remote(block, block, qp_send, qp_recv.at[i], (plane(core, da, db), z)).start()
 
     def q_split(which):
         for from_z in range(16):
@@ -297,32 +287,26 @@
 
     def q_mate(a, b):
         block = q_block(plane(core, a, b))
-        i = index(a, b)
-        copy = remote(block, block, qc_send.at[i], qc_recv.at[i], (sibling, z))
-        copy.start()
-        q_sent.append(copy)
+        remote(block, block, qc_send, qc_recv.at[group[a, b]], (sibling, z)).start()
 
     def q_take(a, b):
         i = index(a, b)
         block = q_block(plane(core, a, b))
-        remote(block, block, qp_send.at[i], qp_recv.at[i], (sibling, z)).wait_recv()
+        wait_bytes(block, qp_recv.at[i])
         q_mate(a, b)
 
-    def q_take_mate(a, b):
-        i = index(a, b)
-        which = plane(1 - core, a, b)
-        remote(q_block(which), q_block(which), qc_send.at[i], qc_recv.at[i], (sibling, z)).wait_recv()
-        q_split(which)
-
-    for piece in near:
-        piece.wait()
+    def q_take_mates(g):
+        wait_bytes(q.at[pl.ds(0, len(groups[g])), pl.ds(0, 32), :], qc_recv.at[g])
+        for a, b in groups[g]:
+            q_split(plane(1 - core, a, b))
+
+    z_wait(2, 11)
     for da, db in ((1, 0), (-1, 0), (2, 0), (0, 1), (0, -1)):
         q_pass(0, 0, da, db)
     q_mate(0, 0)
     q_split(dp)
 
-    for copy in up3 + down3:
-        copy.wait_recv()
+    wait_bytes(third, rs_recv.at[9])
     x = mine + third[0] + third[1]
 
     fin, fout = factors(dot_tn(x, x, HIGHEST))
@@ -352,7 +336,7 @@
     q_take(0, -1)
     for a, b in ((1, 0), (-1, 0), (0, 1), (0, -1), (2, 0)):
         q_split(plane(core, a, b))
-    q_take_mate(0, 0)
+    q_take_mates(0)
 
     def take_all(own, ref, which):
         pltpu.make_async_copy(ref.at[others], ref.at[others], fsum_recv.at[which]).wait()
@@ -368,8 +352,9 @@
     def sent_all(ref, which):
         pltpu.make_async_copy(ref.at[others], ref.at[others], fsum_send.at[which]).wait()
 
-    for copy in stage1 + up2 + down2 + up3 + down3 + [fisher_pair]:
-        copy.wait_send()
+    wait_bytes(part.at[pl.ds(0, 15)], rs_send)
+    fisher_pair.wait_send()
+    wait_bytes(q.at[pl.ds(0, 15), pl.ds(0, 16), pl.ds(0, 128)], qz_send)
     sent_all(fz, 0)
 
     for a in (1, -1):
@@ -379,11 +364,9 @@
         q_take(a, b)
     for a, b in ((1, 1), (-1, 1), (1, -1), (-1, -1), (0, 2), (2, 1), (2, -1)):
         q_split(plane(core, a, b))
-    for a, b in ((1, 0), (-1, 0), (0, 1), (0, -1), (2, 0), (1, 1), (-1, 1), (1, -1), (-1, -1), (0, 2)):
-        q_take_mate(a, b)
-
-    for copy in q_sent[:6]:
-        copy.wait_send()
+    q_take_mates(1)
+    q_take_mates(2)
+
     fisher = unpack(take_all(zsum, fp, 1))
     eye = iota((32, 128), 0) == iota((32, 128), 1)
     fisher = fisher / tokens + jnp.where(eye, damping, 0.0)
@@ -394,8 +377,7 @@
     for a, b in ((2, 2), (1, 2), (-1, 2)):
         q_take(a, b)
         q_split(plane(core, a, b))
-    for a, b in ((2, 1), (2, -1), (2, 2), (1, 2), (-1, 2)):
-        q_take_mate(a, b)
+    q_take_mates(3)
 
     swap.wait_recv()
     mine_inv, other_inv = minv[...], mpair[...]
@@ -422,8 +404,9 @@
 
     lax.fori_loop(0, 4, score, 0)
 
-    for copy in [swap] + q_sent[6:]:
-        copy.wait_send()
+    swap.wait_send()
+    wait_bytes(q.at[pl.ds(0, 15), pl.ds(0, 32), :], qp_send)
+    wait_bytes(q.at[:, pl.ds(0, 32), :], qc_send)
     sent_all(fp, 1)
 
 
@@ -446,9 +429,7 @@
             pltpu.VMEM((16, 128, 256), bf16),
             pltpu.VMEM((128, 2304), bf16),
             pltpu.VMEM((16, 64, 128), f32),
-            pltpu.VMEM((5, 64, 128), f32),
-            pltpu.VMEM((5, 64, 128), f32),
-            pltpu.VMEM((2, 32, 128), f32),
+            pltpu.VMEM((5, 160, 128), f32),
             pltpu.VMEM((2, 64, 128), f32),
             pltpu.VMEM((2, 64, 128), f32),
             pltpu.VMEM((8, 128), f32),
@@ -463,15 +444,15 @@
             pltpu.VMEM((16, 64, 1024), bf16),
             pltpu.VMEM((16, 64, 1024), bf16),
             pltpu.VMEM((1024, 256), bf16),
-            dma((4,)),
+            dma,
             dma((2, 2)),
             dma,
-            dma((20,)), dma((20,)),
+            dma, dma((10,)),
             dma((2,)), dma((2,)),
             dma((2,)), dma((2,)),
-            dma((16,)), dma((16,)),
-            dma((16,)), dma((16,)),
-            dma((16,)), dma((16,)),
+            dma, dma((3,)),
+            dma, dma((16,)),
+            dma, dma((4,)),
         ],
         name="influence",
         compiler_params=pltpu.CompilerParams(

time: 50.2 us -> 49.4 us (0.984)
  Pallas kernels: 49.3 us -> 48.5 us
    pallas_call x1, Pallas kernels: 49.3 us -> 48.5 us  [body(): pl.pallas_call(call, out_shape=pltpu.VMEM((128, 1024), f32), in_specs=[hb...]
where the time goes in v6:
time: 49.4 us; the launch traced here: 49.3 us
  Pallas kernels  48.5 us (98%)
  local copies, waits for them, and re-layouts  0.8 us (2%)
    pallas_call x1, Pallas kernels, body(): pl.pallas_call(call, out_shape=pltpu.VMEM((128, 1024), f32), in_specs=[hb...  48.5 us

profile of v6, /device:TPU:1, one launch (start us, length us, event | category | flops | bytes accessed | tf_op | source)
XLA Modules:
  0.0 49.3 jit_solution(8014244154053243901)
XLA Ops:
  0.0 48.5 %influence.1 = f32[128,1024]{1,0:T(8,128)S(1)} custom-call(bf16[2048,896]{1,0:T(8,128)(2,1)} %refs_0_.1, bf16[2048,256]{1,0:T(8,128)(2,1)} %refs_1_.1, bf16[32,896]{1,0:T(8,128)(2,1)} %bitcast.2, bf16[32,256]{1,0:T(8,128)(2,1)} %bitcast.3, f32[64,1024]{1,0:T(8,128)} %refs_4_.1), custom_call_target="tpu_custom_call" | custom-call | tf_op jit(solution)/shard_map/influence/pallas_call | solution.py:422
  48.5 0.8 %copy.7 = f32[128,1024]{1,0:T(8,128)} copy(f32[128,1024]{1,0:T(8,128)S(1)} %influence.1) | data formatting | bytes 1048576

commit v7 on v6

--- a/solution.py
+++ b/solution.py
@@ -112,20 +112,36 @@
             device_id=device, device_id_type=MESH,
         )
 
+    def wait_bytes(ref, sem):
+        pltpu.make_async_copy(ref, ref, sem).wait()
+
     barrier = pltpu.get_barrier_semaphore()
-
-    def hello_chip(i, carry):
-        pl.semaphore_signal(barrier, inc=1, device_id=(chip(i), z), device_id_type=MESH)
-        return carry
 
     for offset in (3, -3, 2, -2, 1, -1):
         pl.semaphore_signal(barrier, inc=1, device_id=(dp, at_z(offset)), device_id_type=MESH)
-    lax.fori_loop(1, 16, hello_chip, 0)
+    for i in (10, 6, 9, 11, 5, 7, 2, 14, 8, 4, 12, 3, 13, 1, 15):
+        pl.semaphore_signal(barrier, inc=1, device_id=(chip(i), z), device_id_type=MESH)
     pl.semaphore_signal(barrier, inc=1, device_id=(sibling, z), device_id_type=MESH)
 
-    def wait_bytes(ref, sem):
-        pltpu.make_async_copy(ref, ref, sem).wait()
-
+    loads = []
+    chunks = ((0, 7), (7, 9))
+    def start_loads(g):
+        start, count = chunks[g]
+
+        def load(j, carry):
+            rows = pl.ds(pl.multiple_of(at_z(5 + j) * 128, 128), 128)
+            pltpu.make_async_copy(hid.at[rows, :], hbuf.at[j], load_sem.at[g, 0]).start()
+            pltpu.make_async_copy(grd.at[rows, :], gbuf.at[j], load_sem.at[g, 1]).start()
+            return carry
+
+        lax.fori_loop(start, start + count, load, 0)
+        held = pl.ds(start, count)
+        loads.append((
+            pltpu.make_async_copy(hbuf.at[held], hbuf.at[held], load_sem.at[g, 0]),
+            pltpu.make_async_copy(gbuf.at[held], gbuf.at[held], load_sem.at[g, 1]),
+        ))
+
+    start_loads(0)
     weights_in = []
     for half in range(2):
         for src, start, width, at in ((wi, 0, 896, 0), (wo, 896, 256, 32)):
@@ -137,21 +153,7 @@
     proj[...] = jnp.zeros_like(proj)
     for copy in weights_in:
         copy.start()
-    loads = []
-    chunks = ((0, 7), (7, 9))
-    for g, (start, count) in enumerate(chunks):
-        def load(j, carry, g=g):
-            rows = pl.ds(pl.multiple_of(at_z(5 + j) * 128, 128), 128)
-            pltpu.make_async_copy(hid.at[rows, :], hbuf.at[j], load_sem.at[g, 0]).start()
-            pltpu.make_async_copy(grd.at[rows, :], gbuf.at[j], load_sem.at[g, 1]).start()
-            return carry
-
-        lax.fori_loop(start, start + count, load, 0)
-        held = pl.ds(start, count)
-        loads.append((
-            pltpu.make_async_copy(hbuf.at[held], hbuf.at[held], load_sem.at[g, 0]),
-            pltpu.make_async_copy(gbuf.at[held], gbuf.at[held], load_sem.at[g, 1]),
-        ))
+    start_loads(1)
 
     def q_rows(which):
         return pl.ds(pl.multiple_of((which // 8) * 16, 16), 16)

time: 49.4 us -> 49.3 us (level)
  no operation moved by 1% of the time
where the time goes in v7:
time: 49.3 us; the launch traced here: 49.2 us
  Pallas kernels  48.4 us (98%)
  local copies, waits for them, and re-layouts  0.8 us (2%)
    pallas_call x1, Pallas kernels, body(): pl.pallas_call(call, out_shape=pltpu.VMEM((128, 1024), f32), in_specs=[hb...  48.4 us

profile of v7, /device:TPU:1, one launch (start us, length us, event | category | flops | bytes accessed | tf_op | source)
XLA Modules:
  0.0 49.2 jit_solution(11787798741170733329)
XLA Ops:
  0.0 48.4 %influence.1 = f32[128,1024]{1,0:T(8,128)S(1)} custom-call(bf16[2048,896]{1,0:T(8,128)(2,1)} %refs_0_.1, bf16[2048,256]{1,0:T(8,128)(2,1)} %refs_1_.1, bf16[32,896]{1,0:T(8,128)(2,1)} %bitcast.2, bf16[32,256]{1,0:T(8,128)(2,1)} %bitcast.3, f32[64,1024]{1,0:T(8,128)} %refs_4_.1), custom_call_target="tpu_custom_call" | custom-call | tf_op jit(solution)/shard_map/influence/pallas_call | solution.py:424
  48.4 0.8 %copy.7 = f32[128,1024]{1,0:T(8,128)} copy(f32[128,1024]{1,0:T(8,128)S(1)} %influence.1) | data formatting | bytes 1048576
